TPU v7x, 32 devices: a whole 2x2x4 slice. The times are simulated.
32 devices in a mesh: dp: 8 (over y, x, core), rows: 4 (over z).
Axes of the slice: x: 2, y: 2, z: 4, core: 2. Of those that a mesh axis runs over, the one named last changes fastest.
Arguments:
- tokens: bfloat16 [32, 28, 70, 384], P('dp', 'rows'), may hold values from -6 to 6
- heights: int32 [32], P('dp'), may hold values from 1 to 4, as said below
- conv_weight: bfloat16 [4, 3, 3, 384], replicated, may hold values from -2 to 2
- conv_bias: bfloat16 [4, 384], replicated, may hold values from -1.5 to 1.5
- norm_gain: bfloat16 [4, 384], replicated, may hold values from 0.5 to 1.5
- norm_shift: bfloat16 [4, 384], replicated, may hold values from -1 to 1
- mix_weight: bfloat16 [2, 384, 1152], replicated, may hold values from -0.3125 to 0.3125
- window_bias: bfloat16 [768], replicated, may hold values from -1.5 to 1.5
- channel_bias: bfloat16 [1152], replicated, may hold values from -0.5 to 0.5
- out_weight: bfloat16 [2, 384, 384], replicated, may hold values from -0.875 to 0.875
- out_bias: bfloat16 [2, 384], replicated, may hold values from -1.5 to 1.5
- up_weight: bfloat16 [2, 384, 1536], replicated, may hold values from -0.3125 to 0.3125
- up_bias: bfloat16 [2, 1536], replicated, may hold values from -1.5 to 1.5
- down_weight: bfloat16 [2, 1536, 384], replicated, may hold values from -0.15625 to 0.15625
- down_bias: bfloat16 [2, 384], replicated, may hold values from -1.5 to 1.5
- cotangent: bfloat16 [32, 28, 70, 384], P('dp', 'rows'), may hold values from -6 to 6
Outputs:
- result: bfloat16 [32, 28, 70, 384], P('dp', 'rows')
- tokens_grad: float32 [32, 28, 70, 384], P('dp', 'rows')
- conv_weight_grad: float32 [4, 3, 3, 384], replicated
- conv_bias_grad: float32 [4, 384], replicated
- norm_gain_grad: float32 [4, 384], replicated
- norm_shift_grad: float32 [3, 384], replicated
- final_shift_grad: float32 [384], replicated
- mix_weight_grad: float32 [2, 384, 1152], replicated
- window_bias_grad: float32 [768], replicated
- channel_bias_grad: float32 [1152], replicated
- out_weight_grad: float32 [2, 384, 384], replicated
- out_bias_grad: float32 [2, 384], replicated
- up_weight_grad: float32 [2, 384, 1536], replicated
- up_bias_grad: float32 [2, 1536], replicated
- down_weight_grad: float32 [2, 1536, 384], replicated
- down_bias_grad: float32 [2, 384], replicated
Inputs may be any that keep to these rules, and one draw needn't show every extreme that they name: `heights`: in each block of 4 images of one index of dp, one image is 4 window rows tall.
All inputs are finite; a program needn't handle non-finite values.
Results may differ from a plain program's by a relative error of at most 0.019.
Values may be sent and summed in bfloat16 or wider, within the bound.
No kernel may reach another device: no remote copies, remote signals or barrier semaphores. Data moves between devices by JAX's collectives and lax.ppermute only.
A program may use at most 320 MiB of HBM per device.

v0:
```python
import jax
import jax.numpy as jnp
from jax import lax
from jax.sharding import PartitionSpec as P

HEADS = 12
HEAD_DIM = 32


EPS = 1e-05
HIGH = lax.Precision.HIGHEST


def with_halo(cells, sides, width):
    for axis, dim in sides:
        count = lax.axis_size(axis)
        ends = count - 1
        head = lax.slice_in_dim(cells, 0, width, axis=dim)
        tail = lax.slice_in_dim(cells, cells.shape[dim] - width, cells.shape[dim], axis=dim)
        cells = jnp.concatenate(
            [
                lax.ppermute(tail, axis, [(i, (i + 1) % count) for i in range(ends)]),
                cells,
                lax.ppermute(head, axis, [((i + 1) % count, i) for i in range(ends)]),
            ],
            axis=dim,
        )
    return cells


def layer_norm(value, gain, shift):
    centre = value - jnp.mean(value, axis=-1, keepdims=True)
    spread = jnp.mean(centre * centre, axis=-1, keepdims=True)
    return centre * lax.rsqrt(spread + EPS) * gain + shift


def gelu_exact(value):
    return jax.nn.gelu(value, approximate=False)


def outer_sum(left, right):
    return jnp.einsum("ta,tb->ab", left, right, preferred_element_type=jnp.float32)


def shifted_sum(padded, weight, height, width, flipped):
    total = jnp.zeros((padded.shape[0], height, width, padded.shape[3]), jnp.float32)
    for row_off in range(3):
        for col_off in range(3):
            start_row = 2 - row_off if flipped else row_off
            start_col = 2 - col_off if flipped else col_off
            total = (
                total
                + padded[:, start_row : start_row + height, start_col : start_col + width]
                * weight[row_off, col_off]
            )
    return total


def position_forward(state, weight, bias, region):
    height, width = (state.shape[1], state.shape[2])
    rounded = state.astype(jnp.bfloat16)
    padded = with_halo(rounded, (("rows", 1),), 1)
    padded = jnp.pad(padded, ((0, 0), (0, 0), (1, 1), (0, 0))).astype(jnp.float32)
    convolved = shifted_sum(padded, weight, height, width, False)
    return (region * (state + convolved + bias), padded)


def position_backward(grad, padded, weight, region):
    height, width, chans = (grad.shape[1], grad.shape[2], grad.shape[3])
    masked = region * grad
    bias_grad = jnp.sum(masked, axis=(0, 1, 2))
    rounded = masked.astype(jnp.bfloat16)
    rounded_wide = rounded.astype(jnp.float32)
    pieces = []
    for row_off in range(3):
        for col_off in range(3):
            window_part = padded[:, row_off : row_off + height, col_off : col_off + width]
            pieces.append(jnp.sum(window_part * rounded_wide, axis=(0, 1, 2)))
    weight_grad = jnp.stack(pieces).reshape(3, 3, chans)
    grad_pad = with_halo(rounded, (("rows", 1),), 1)
    grad_pad = jnp.pad(grad_pad, ((0, 0), (0, 0), (1, 1), (0, 0))).astype(jnp.float32)
    return (masked + shifted_sum(grad_pad, weight, height, width, True), weight_grad, bias_grad)


def to_windows(flat, images, height, width):
    blocks = flat.reshape(images, height // 7, 7, width // 7, 7, HEADS, HEAD_DIM)
    return blocks.transpose(0, 1, 3, 5, 2, 4, 6).reshape(-1, HEADS, 49, HEAD_DIM)


def from_windows(windows, images, height, width):
    blocks = windows.reshape(images, height // 7, width // 7, HEADS, 7, 7, HEAD_DIM)
    return blocks.transpose(0, 1, 4, 2, 5, 3, 6).reshape(images * height * width, HEADS * HEAD_DIM)


def window_probs(query, key):
    scores = jnp.einsum(
        "nhqd,nhkd->nhqk", query, key, preferred_element_type=jnp.float32
    ) * HEAD_DIM ** (-0.5)
    return jax.nn.softmax(scores, axis=-1)


def norm_backward(state, gain, shift, normed_grad):
    _, pull = jax.vjp(layer_norm, state, gain, shift)
    return pull(normed_grad.reshape(state.shape))


def window_forward(state, gain, shift, weight, bias_full, out_w, out_b, region):
    images, height, width, chans = state.shape
    normed = layer_norm(state, gain, shift).astype(jnp.bfloat16).reshape(-1, chans)
    mixed = (jnp.dot(normed, weight, preferred_element_type=jnp.float32) + bias_full).astype(
        jnp.bfloat16
    )
    query = to_windows(mixed[:, :chans], images, height, width)
    key = to_windows(mixed[:, chans : 2 * chans], images, height, width)
    value = to_windows(mixed[:, 2 * chans :], images, height, width)
    probs = window_probs(query, key).astype(jnp.bfloat16)
    attended = jnp.einsum(
        "nhqk,nhkd->nhqd", probs, value, preferred_element_type=jnp.float32
    ).astype(jnp.bfloat16)
    merged = from_windows(attended, images, height, width)
    branch = jnp.dot(merged, out_w, preferred_element_type=jnp.float32) + out_b
    return (region * (state + branch.reshape(state.shape)), (normed, mixed, merged))


def window_backward(grad, state, kept, gain, shift, weight, out_w, region):
    images, height, width, chans = state.shape
    normed, mixed, merged = kept
    masked = region * grad
    flat = masked.reshape(-1, chans)
    out_b_grad = jnp.sum(flat, axis=0)
    rounded = flat.astype(jnp.bfloat16)
    out_w_grad = outer_sum(merged, rounded)
    merged_grad = jnp.dot(rounded, out_w.T, preferred_element_type=jnp.float32).astype(jnp.bfloat16)
    attended_grad = to_windows(merged_grad, images, height, width)
    query = to_windows(mixed[:, :chans], images, height, width)
    key = to_windows(mixed[:, chans : 2 * chans], images, height, width)
    value = to_windows(mixed[:, 2 * chans :], images, height, width)
    probs = window_probs(query, key)
    value_grad = jnp.einsum(
        "nhqk,nhqd->nhkd",
        probs.astype(jnp.bfloat16),
        attended_grad,
        preferred_element_type=jnp.float32,
    )
    prob_grad = jnp.einsum(
        "nhqd,nhkd->nhqk", attended_grad, value, preferred_element_type=jnp.float32
    )
    score_grad = probs * (prob_grad - jnp.sum(prob_grad * probs, axis=-1, keepdims=True))
    score_low = score_grad.astype(jnp.bfloat16)
    query_grad = jnp.einsum(
        "nhqk,nhkd->nhqd", score_low, key, preferred_element_type=jnp.float32
    ) * HEAD_DIM ** (-0.5)
    key_grad = jnp.einsum(
        "nhqk,nhqd->nhkd", score_low, query, preferred_element_type=jnp.float32
    ) * HEAD_DIM ** (-0.5)
    mixed_grad = jnp.concatenate(
        [
            from_windows(query_grad, images, height, width),
            from_windows(key_grad, images, height, width),
            from_windows(value_grad, images, height, width),
        ],
        axis=1,
    )
    bias_grad = jnp.concatenate(
        [jnp.sum(mixed_grad[:, :chans], axis=0), jnp.sum(mixed_grad[:, 2 * chans :], axis=0)]
    )
    mixed_low = mixed_grad.astype(jnp.bfloat16)
    mix_w_grad = outer_sum(normed, mixed_low)
    normed_grad = jnp.dot(mixed_low, weight.T, preferred_element_type=jnp.float32)
    state_grad, gain_grad, shift_grad = norm_backward(state, gain, shift, normed_grad)
    return (
        masked + state_grad,
        gain_grad,
        shift_grad,
        mix_w_grad,
        bias_grad,
        out_w_grad,
        out_b_grad,
    )


def channel_forward(state, gain, shift, weight, bias, out_w, out_b, region, keep_tok, scale):
    images, height, width, chans = state.shape
    normed = layer_norm(state, gain, shift).astype(jnp.bfloat16).reshape(-1, chans)
    mixed = (jnp.dot(normed, weight, preferred_element_type=jnp.float32) + bias).astype(
        jnp.bfloat16
    )
    grouped = mixed.reshape(images, -1, 3, HEADS, HEAD_DIM)
    key = grouped[:, :, 1] * keep_tok
    partial_gram = jnp.einsum(
        "ithd,ithe->ihde", key, grouped[:, :, 2], preferred_element_type=jnp.float32
    )
    gram = lax.psum(partial_gram, "rows")
    weights = jax.nn.softmax(gram * scale[:, None, None, None], axis=-1)
    attended = jnp.einsum(
        "ihde,ithe->ithd",
        weights.astype(jnp.bfloat16),
        grouped[:, :, 0],
        preferred_element_type=jnp.float32,
    )
    merged = attended.astype(jnp.bfloat16).reshape(-1, chans)
    branch = jnp.dot(merged, out_w, preferred_element_type=jnp.float32) + out_b
    return (region * (state + branch.reshape(state.shape)), (normed, mixed, weights, merged))


def channel_backward(grad, state, kept, gain, shift, weight, out_w, region, keep_tok, scale):
    images, height, width, chans = state.shape
    normed, mixed, weights, merged = kept
    masked = region * grad
    flat = masked.reshape(-1, chans)
    out_b_grad = jnp.sum(flat, axis=0)
    rounded = flat.astype(jnp.bfloat16)
    out_w_grad = outer_sum(merged, rounded)
    attended_grad = jnp.dot(rounded, out_w.T, preferred_element_type=jnp.float32).astype(
        jnp.bfloat16
    )
    attended_grad = attended_grad.reshape(images, -1, HEADS, HEAD_DIM)
    grouped = mixed.reshape(images, -1, 3, HEADS, HEAD_DIM)
    query = grouped[:, :, 0]
    key = (grouped[:, :, 1] * keep_tok).astype(jnp.float32)
    value = grouped[:, :, 2].astype(jnp.float32)
    query_grad = jnp.einsum(
        "ihde,ithd->ithe",
        weights.astype(jnp.bfloat16),
        attended_grad,
        preferred_element_type=jnp.float32,
    )
    partial_grad = jnp.einsum(
        "ithd,ithe->ihde", attended_grad, query, preferred_element_type=jnp.float32
    )
    weights_grad = lax.psum(partial_grad, "rows")
    logit_grad = weights * (weights_grad - jnp.sum(weights_grad * weights, axis=-1, keepdims=True))
    gram_grad = logit_grad.astype(jnp.bfloat16).astype(jnp.float32) * scale[:, None, None, None]
    key_grad = jnp.einsum("ihde,ithe->ithd", gram_grad, value, precision=HIGH) * keep_tok.astype(
        jnp.float32
    )
    value_grad = jnp.einsum("ihde,ithd->ithe", gram_grad, key, precision=HIGH)
    mixed_grad = jnp.stack([query_grad, key_grad, value_grad], axis=2).reshape(-1, 3 * chans)
    bias_grad = jnp.sum(mixed_grad, axis=0)
    mixed_low = mixed_grad.astype(jnp.bfloat16)
    mix_w_grad = outer_sum(normed, mixed_low)
    normed_grad = jnp.dot(mixed_low, weight.T, preferred_element_type=jnp.float32)
    state_grad, gain_grad, shift_grad = norm_backward(state, gain, shift, normed_grad)
    return (
        masked + state_grad,
        gain_grad,
        shift_grad,
        mix_w_grad,
        bias_grad,
        out_w_grad,
        out_b_grad,
    )


def mlp_forward(state, gain, shift, up_w, up_b, down_w, down_b, region):
    chans = state.shape[-1]
    normed = layer_norm(state, gain, shift).astype(jnp.bfloat16).reshape(-1, chans)
    pre_act = jnp.dot(normed, up_w, preferred_element_type=jnp.float32) + up_b
    hidden = gelu_exact(pre_act).astype(jnp.bfloat16)
    branch = jnp.dot(hidden, down_w, preferred_element_type=jnp.float32) + down_b
    return (region * (state + branch.reshape(state.shape)), (normed, pre_act, hidden))


def mlp_backward(grad, state, kept, gain, shift, up_w, down_w, region):
    chans = state.shape[-1]
    normed, pre_act, hidden = kept
    masked = region * grad
    flat = masked.reshape(-1, chans)
    down_b_grad = jnp.sum(flat, axis=0)
    rounded = flat.astype(jnp.bfloat16)
    down_w_grad = outer_sum(hidden, rounded)
    hidden_grad = jnp.dot(rounded, down_w.T, preferred_element_type=jnp.float32)
    _, pull = jax.vjp(gelu_exact, pre_act)
    pre_grad = pull(hidden_grad)[0]
    up_b_grad = jnp.sum(pre_grad, axis=0)
    pre_low = pre_grad.astype(jnp.bfloat16)
    up_w_grad = outer_sum(normed, pre_low)
    normed_grad = jnp.dot(pre_low, up_w.T, preferred_element_type=jnp.float32)
    state_grad, gain_grad, shift_grad = norm_backward(state, gain, shift, normed_grad)
    return (
        masked + state_grad,
        gain_grad,
        shift_grad,
        up_w_grad,
        up_b_grad,
        down_w_grad,
        down_b_grad,
    )


def local(
    tokens,
    heights,
    conv_weight,
    conv_bias,
    norm_gain,
    norm_shift,
    mix_weight,
    window_bias,
    channel_bias,
    out_weight,
    out_bias,
    up_weight,
    up_bias,
    down_weight,
    down_bias,
    cotangent,
):
    images, height, width, chans = tokens.shape
    row_ids = lax.axis_index("rows") * height + jnp.arange(height, dtype=jnp.int32)
    region = (row_ids[None, :] < heights[:, None] * 7).astype(jnp.float32)[:, :, None, None]
    keep_tok = (
        jnp.broadcast_to(region, (images, height, width, 1))
        .reshape(images, -1, 1, 1)
        .astype(jnp.bfloat16)
    )
    scale = lax.rsqrt((heights * 7 * width).astype(jnp.float32))
    conv_w = conv_weight.astype(jnp.float32)
    conv_b = conv_bias.astype(jnp.float32)
    gain = norm_gain.astype(jnp.float32)
    shift = norm_shift.astype(jnp.float32)
    win_b = window_bias.astype(jnp.float32)
    bias_full = jnp.concatenate([win_b[:chans], jnp.zeros((chans,), jnp.float32), win_b[chans:]])
    chan_b = channel_bias.astype(jnp.float32)
    out_b = out_bias.astype(jnp.float32)
    up_b = up_bias.astype(jnp.float32)
    down_b = down_bias.astype(jnp.float32)
    state_zero = region * tokens.astype(jnp.float32)
    state_one, pad_one = position_forward(state_zero, conv_w[0], conv_b[0], region)
    state_two, kept_two = window_forward(
        state_one, gain[0], shift[0], mix_weight[0], bias_full, out_weight[0], out_b[0], region
    )
    state_three, pad_three = position_forward(state_two, conv_w[1], conv_b[1], region)
    state_four, kept_four = mlp_forward(
        state_three, gain[1], shift[1], up_weight[0], up_b[0], down_weight[0], down_b[0], region
    )
    state_five, pad_five = position_forward(state_four, conv_w[2], conv_b[2], region)
    state_six, kept_six = channel_forward(
        state_five,
        gain[2],
        shift[2],
        mix_weight[1],
        chan_b,
        out_weight[1],
        out_b[1],
        region,
        keep_tok,
        scale,
    )
    state_seven, pad_seven = position_forward(state_six, conv_w[3], conv_b[3], region)
    state_eight, kept_eight = mlp_forward(
        state_seven, gain[3], shift[3], up_weight[1], up_b[1], down_weight[1], down_b[1], region
    )
    result = state_eight.astype(jnp.bfloat16)
    grad = cotangent.astype(jnp.float32)
    grad, gain_g3, shift_g3, up_wg1, up_bg1, down_wg1, down_bg1 = mlp_backward(
        grad, state_seven, kept_eight, gain[3], shift[3], up_weight[1], down_weight[1], region
    )
    grad, conv_wg3, conv_bg3 = position_backward(grad, pad_seven, conv_w[3], region)
    grad, gain_g2, shift_g2, mix_wg1, chan_bg, out_wg1, out_bg1 = channel_backward(
        grad,
        state_five,
        kept_six,
        gain[2],
        shift[2],
        mix_weight[1],
        out_weight[1],
        region,
        keep_tok,
        scale,
    )
    grad, conv_wg2, conv_bg2 = position_backward(grad, pad_five, conv_w[2], region)
    grad, gain_g1, shift_g1, up_wg0, up_bg0, down_wg0, down_bg0 = mlp_backward(
        grad, state_three, kept_four, gain[1], shift[1], up_weight[0], down_weight[0], region
    )
    grad, conv_wg1, conv_bg1 = position_backward(grad, pad_three, conv_w[1], region)
    grad, gain_g0, shift_g0, mix_wg0, win_bg, out_wg0, out_bg0 = window_backward(
        grad, state_one, kept_two, gain[0], shift[0], mix_weight[0], out_weight[0], region
    )
    grad, conv_wg0, conv_bg0 = position_backward(grad, pad_one, conv_w[0], region)
    tokens_grad = region * grad
    conv_w_grad = jnp.stack([conv_wg0, conv_wg1, conv_wg2, conv_wg3])
    conv_b_grad = jnp.stack([conv_bg0, conv_bg1, conv_bg2, conv_bg3])
    gain_grad = jnp.stack([gain_g0, gain_g1, gain_g2, gain_g3])
    shift_grad = jnp.stack([shift_g0, shift_g1, shift_g2])
    final_shift = shift_g3
    mix_w_grad = jnp.stack([mix_wg0, mix_wg1])
    out_w_grad = jnp.stack([out_wg0, out_wg1])
    out_b_grad = jnp.stack([out_bg0, out_bg1])
    up_w_grad = jnp.stack([up_wg0, up_wg1])
    up_b_grad = jnp.stack([up_bg0, up_bg1])
    down_w_grad = jnp.stack([down_wg0, down_wg1])
    down_b_grad = jnp.stack([down_bg0, down_bg1])
    summed = lax.psum(
        (
            conv_w_grad,
            conv_b_grad,
            gain_grad,
            shift_grad,
            final_shift,
            mix_w_grad,
            win_bg,
            chan_bg,
            out_w_grad,
            out_b_grad,
            up_w_grad,
            up_b_grad,
            down_w_grad,
            down_b_grad,
        ),
        ("dp", "rows"),
    )
    (
        conv_w_grad,
        conv_b_grad,
        gain_grad,
        shift_grad,
        final_shift,
        mix_w_grad,
        win_bg,
        chan_bg,
        out_w_grad,
        out_b_grad,
        up_w_grad,
        up_b_grad,
        down_w_grad,
        down_b_grad,
    ) = summed
    return (
        result,
        tokens_grad,
        conv_w_grad,
        conv_b_grad,
        gain_grad,
        shift_grad,
        final_shift,
        mix_w_grad,
        win_bg,
        chan_bg,
        out_w_grad,
        out_b_grad,
        up_w_grad,
        up_b_grad,
        down_w_grad,
        down_b_grad,
    )


def solution(mesh):
    in_specs = (
        P("dp", "rows", None, None),
        P("dp"),
        P(),
        P(),
        P(),
        P(),
        P(),
        P(),
        P(),
        P(),
        P(),
        P(),
        P(),
        P(),
        P(),
        P("dp", "rows", None, None),
    )
    out_specs = (
        P("dp", "rows", None, None),
        P("dp", "rows", None, None),
        P(),
        P(),
        P(),
        P(),
        P(),
        P(),
        P(),
        P(),
        P(),
        P(),
        P(),
        P(),
        P(),
        P(),
    )
    return jax.shard_map(local, mesh=mesh, in_specs=in_specs, out_specs=out_specs, check_vma=False)
```

profile of v0, /device:TPU:0, one launch (start us, length us, event | category | flops | bytes accessed | tf_op | source)
XLA Modules:
  0.0 1476.0 jit_solution(13104498325760646879)
XLA Ops:
  41.3 9.9 reshape.398
  59.1 11.3 reshape.399
  70.4 9.9 reshape.400
  88.2 11.3 reshape.401
  99.5 10.2 reshape.402
  117.6 11.3 reshape.403
  128.9 14.2 fusion.248
  143.1 10.2 fusion.124
  153.3 8.5 copy.108
  161.8 11.5 reshape.404
  173.3 8.1 copy.109
  181.4 10.1 reshape.405
  226.6 31.0 %multiply_convert_fusion.2 = (bf16[1960,1536]{1,0:T(8,128)(2,1)S(1)}, f32[1960,1536]{1,0:T(8,128)}, f32[1960,1536]{1,0:T(8,128)}) fusion(f32[1536]{0:T(1024)S(1)} %get-tuple-element.153, bf16[1960,384]{1,0:T(8,128)(2,1)} %reshape.407, bf16[2,384,1536]{2,1,0:T(8,128)(2,1)} %param.27), kind=kOutput, calls=%fused_computation.31 | convolution fusion | flops 2510807040 | bytes 32796672 | tf_op jit(solution)/shard_map/dot_general | solution.py:258
  307.1 10.3 reshape.410
  327.1 41.9 %all-reduce.15.cloned.1.call-done = f32[4,12,32,32]{3,2,1,0:T(8,128)} async-done(((f32[4,12,32,32]{3,2,1,0:T(8,128)}), f32[4,12,32,32]{3,2,1,0:T(8,128)}) %all-reduce.15.cloned.1.call-update) | async-done | bytes 196624 | tf_op jit(solution)/shard_map/psum | solution.py:193
  413.1 31.0 %multiply_convert_fusion.1 = (bf16[1960,1536]{1,0:T(8,128)(2,1)}, f32[1960,1536]{1,0:T(8,128)}, f32[1960,1536]{1,0:T(8,128)}) fusion(f32[1536]{0:T(1024)S(1)} %copy-done.194, bf16[1960,384]{1,0:T(8,128)(2,1)S(1)} %reshape.413, bf16[2,384,1536]{2,1,0:T(8,128)(2,1)} %param.27), kind=kOutput, calls=%fused_computation.18 | convolution fusion | flops 2510807040 | bytes 32796672 | tf_op jit(solution)/shard_map/dot_general | solution.py:258
  444.2 14.9 %fusion.235 = (f32[1536]{0:T(1024)S(1)}, bf16[1960,1536]{1,0:T(8,128)(2,1)}) fusion(f32[1960,1536]{1,0:T(8,128)} %get-tuple-element.203, bf16[1960,384]{1,0:T(8,128)(2,1)S(1)} %copy-done.71, bf16[2,1536,384]{2,1,0:T(8,128)(2,1)S(1)} %copy-done.226, f32[1960,1536]{1,0:T(8,128)} %get-tuple-element.256, f32[1536]{0:T(1024)S(1)} %copy-done.194), kind=kOutput, calls=%fused_computation.490 | convolution fusion | flops 2360277504 | bytes 32804864 | tf_op jit(solution)/shard_map/dot_general | solution.py:272
  459.0 8.6 dot_general.126
  541.7 39.5 %all-reduce.17.cloned.1.call-done = f32[4,12,32,32]{3,2,1,0:T(8,128)} async-done(((f32[4,12,32,32]{3,2,1,0:T(8,128)}), f32[4,12,32,32]{3,2,1,0:T(8,128)}) %all-reduce.17.cloned.1.call-update) | async-done | bytes 196624 | tf_op jit(solution)/shard_map/psum | solution.py:231
  581.3 10.3 fusion.149
  606.1 14.5 convert_element_type.301
  620.6 8.3 fusion.217
  643.7 10.5 convert_element_type.319
  679.8 12.5 fusion.234
  699.0 8.6 dot_general.135
  766.7 11.4 reshape.417
  778.1 16.0 %multiply_reduce_fusion = (f32[40,12,49]{2,1,0:T(8,128)S(1)}, f32[40,12,49,49]{2,3,1,0:T(8,128)}) fusion(f32[40,12,49,49]{2,3,1,0:T(8,128)} %get-tuple-element.252, f32[40,12,49]{2,1,0:T(8,128)S(1)} %copy-done.84, bf16[40,12,49,32]{3,2,1,0:T(8,128)(2,1)} %reshape.417, bf16[40,12,49,32]{3,2,1,0:T(8,128)(2,1)} %reshape.403), kind=kOutput, calls=%fused_computation.6 | convolution fusion | flops 77192640 | bytes 12418560 | tf_op jit(solution)/shard_map/nhqd,nhkd->nhqk/dot_general | solution.py:145
  794.1 12.6 multiply_convert_fusion
  806.8 10.1 broadcast_multiply_fusion
  816.9 10.5 multiply_convert_fusion.3
  827.4 15.7 %fusion.38 = f32[40,12,49,32]{3,2,1,0:T(8,128)} fusion(bf16[40,12,49,32]{3,2,1,0:T(8,128)(2,1)} %reshape.417, f32[40,12,49,49]{2,3,1,0:T(8,128)} %get-tuple-element.252, f32[40,12,49]{2,1,0:T(8,128)S(1)} %copy-done.84), kind=kOutput, calls=%fused_computation.117 | convolution fusion | flops 76063680 | bytes 9219840 | tf_op jit(solution)/shard_map/nhqk,nhqd->nhkd/dot_general | solution.py:139
  843.1 11.6 copy.129
  854.7 15.4 %reshape.418 = f32[4,1,10,12,7,7,32]{6,5,4,3,2,0,1:T(8,128)} reshape(f32[40,12,49,32]{3,2,1,0:T(8,128)} %copy.129) | data formatting | bytes 6021120 | tf_op jit(solution)/shard_map/reshape | solution.py:91
  870.1 15.4 %copy.207 = bf16[4,1,10,12,7,7,32]{6,0,3,5,2,4,1:T(4,128)(2,1)} copy(f32[4,1,10,12,7,7,32]{6,5,4,3,2,0,1:T(8,128)} %reshape.418) | data formatting | bytes 4515840 | tf_op jit(solution)/shard_map/reshape | solution.py:91
  885.5 13.1 bitcast_reduce_fusion.1
  898.6 15.5 %reshape.420 = f32[4,1,10,12,7,7,32]{6,5,4,3,2,0,1:T(8,128)} reshape(f32[40,12,49,32]{3,2,1,0:T(8,128)} %fusion.38) | data formatting | bytes 6021120 | tf_op jit(solution)/shard_map/reshape | solution.py:91
  914.1 15.7 %copy.206 = bf16[4,1,10,12,7,7,32]{6,0,3,5,2,4,1:T(4,128)(2,1)} copy(f32[4,1,10,12,7,7,32]{6,5,4,3,2,0,1:T(8,128)} %reshape.420) | data formatting | bytes 4515840 | tf_op jit(solution)/shard_map/reshape | solution.py:91
  929.8 13.1 bitcast_reduce_fusion
  950.0 10.1 reshape.421
  960.1 9.4 concatenate.52
  969.5 8.5 copy.134
  978.0 11.6 reshape.424
  997.7 10.1 reshape.422
  1007.7 9.4 concatenate.53
  1024.3 10.1 reshape.423
  1034.4 9.5 concatenate.54
  1077.8 118.9 %all-reduce.19.cloned.1.call-done = (f32[4,3,3,384]{3,2,1,0:T(4,128)}, f32[4,384]{1,0:T(4,128)}, f32[4,384]{1,0:T(4,128)}, f32[3,384]{1,0:T(4,128)}, f32[384]{0:...) async-done(((f32[4,3,3,384]{3,2,1,0:T(4,128)}, f32[4,384]{1,0:T(4,128)}, f32[4,384]{1,0:T(4,128)}, ...) | async-done | bytes 99856 | tf_op jit(solution)/shard_map/psum | solution.py:394
  1206.5 246.8 %all-reduce.21.cloned.1.call-done = (f32[2,384,1152]{2,1,0:T(8,128)}, f32[2,384,384]{2,1,0:T(8,128)}, f32[2,384,1536]{2,1,0:T(8,128)}, f32[2,1536,384]{2,1,0:T(8,128)}) async-done(((f32[2,384,1152]{2,1,0:T(8,128)}, f32[2,384,384]{2,1,0:T(8,128)}, f32[2,384,1536]{2,1,0:T(8,128)}, f32[2,1536,384]{2,1,0:T(8,128)}), (f32[2,384,1152]{2,1,0:T(8,128)}, f32[2,384,384]{2,1,0:T(8,128)}, f32[2,384,1536]{2,1,0:T(8,128)}, ...) | async-done | bytes 14155792 | tf_op jit(solution)/shard_map/psum | solution.py:394
  (768 shorter events, 469.8 us)
Async XLA Ops:
  7.3 12.2 copy-start.222
  7.3 361.8 %all-reduce.15.cloned.1.call-start = ((), (), s32[]{:S(2)}) async-start(), calls=%async_computation | async-start | bytes 1572864 | tf_op jit(solution)/shard_map/psum | solution.py:193
  8.6 730.4 %copy-start.74 = (f32[4,7]{1,0:T(4,128)}, f32[4,7]{1,0:T(4,128)S(1)}, u32[]{:S(2)}) copy-start(f32[4,7]{1,0:T(4,128)S(1)} %get-tuple-element.250) | copy-start | bytes 340
  10.5 9.6 collective-permute-start
  15.4 8.8 collective-permute-start.1
  19.5 207.1 %copy-start.192 = (f32[1536]{0:T(1024)}, f32[1536]{0:T(1024)S(1)}, u32[]{:S(2)}) copy-start(f32[1536]{0:T(1024)S(1)} %get-tuple-element.153) | copy-start | bytes 18436
  20.1 201.7 %copy-start.105 = (f32[384]{0:T(512)}, f32[384]{0:T(512)S(1)}, u32[]{:S(2)}) copy-start(f32[384]{0:T(512)S(1)} %get-tuple-element.270) | copy-start | bytes 4612
  29.0 170.4 %copy-start.13 = (f32[4,7,70,384]{3,2,1,0:T(8,128)}, f32[4,7,70,384]{3,2,1,0:T(8,128)S(1)}, u32[]{:S(2)}) copy-start(f32[4,7,70,384]{3,2,1,0:T(8,128)S(1)} %get-tuple-element.213) | copy-start | bytes 9031684
  204.4 7.2 collective-permute-start.2
  208.2 7.8 collective-permute-start.3
  220.9 66.6 %copy-start.8 = (f32[4,7,70,384]{3,2,1,0:T(8,128)}, f32[4,7,70,384]{3,2,1,0:T(8,128)S(1)}, u32[]{:S(2)}) copy-start(f32[4,7,70,384]{3,2,1,0:T(8,128)S(1)} %get-tuple-element.211) | copy-start | bytes 9031684
  226.6 33.6 %copy-start.225 = (bf16[2,1536,384]{2,1,0:T(8,128)(2,1)S(1)}, bf16[2,1536,384]{2,1,0:T(8,128)(2,1)}, u32[]{:S(2)}) copy-start(bf16[2,1536,384]{2,1,0:T(8,128)(2,1)} %param.29) | copy-start | bytes 7077892
  273.2 14.3 copy-start.190
  273.2 7.4 collective-permute-start.4
  277.5 7.9 collective-permute-start.5
  320.8 50.8 %copy-start.67 = (bf16[4,490,1,12,32]{1,0,4,3,2:T(4,128)(2,1)}, bf16[4,490,1,12,32]{1,0,4,3,2:T(4,128)(2,1)S(1)}, u32[]{:S(2)}) copy-start(bf16[4,490,1,12,32]{1,0,4,3,2:T(4,128)(2,1)S(1)} %get-tuple-element.219) | copy-start | bytes 4515844
  327.0 254.2 %all-reduce.17.cloned.1.call-start = ((), (), s32[]{:S(2)}) async-start(), calls=%async_computation.1 | async-start | bytes 1572864 | tf_op jit(solution)/shard_map/psum | solution.py:231
  327.1 44.5 %copy-start.223 = (f32[4]{0:T(128)}, f32[4]{0:T(128)S(1)}, u32[]{:S(2)}) copy-start(f32[4]{0:T(128)S(1)} %convert_rsqrt_fusion) | copy-start | bytes 52
  391.5 9.7 collective-permute-start.6
  395.3 8.7 collective-permute-start.7
  413.1 31.1 %copy-start.45 = (bf16[1960,384]{1,0:T(8,128)(2,1)}, bf16[1960,384]{1,0:T(8,128)(2,1)S(1)}, u32[]{:S(2)}) copy-start(bf16[1960,384]{1,0:T(8,128)(2,1)S(1)} %reshape.413) | copy-start | bytes 4515844
  413.1 31.1 %copy-start.71 = (bf16[1960,384]{1,0:T(8,128)(2,1)S(1)}, bf16[1960,384]{1,0:T(8,128)(2,1)}, u32[]{:S(2)}) copy-start(bf16[1960,384]{1,0:T(8,128)(2,1)} %convert_element_type.290) | copy-start | bytes 4515844
  413.1 31.1 %copy-start.226 = (bf16[2,1536,384]{2,1,0:T(8,128)(2,1)S(1)}, bf16[2,1536,384]{2,1,0:T(8,128)(2,1)}, u32[]{:S(2)}) copy-start(bf16[2,1536,384]{2,1,0:T(8,128)(2,1)} %param.29) | copy-start | bytes 7077892
  493.8 15.7 %slice-start = ((s8[6021120]{0:T(1024)(128)(4,1)}), s8[4194304]{0:T(1024)(128)(4,1)S(1)}, s32[]{:S(2)}) async-start(s8[6021120]{0:T(1024)(128)(4,1)} %bitcast.213), calls=%async_computation.4 | async-start | bytes 8388608
  505.0 10.6 collective-permute-start.8
  508.0 8.0 collective-permute-start.9
  537.3 659.4 %all-reduce.19.cloned.1.call-start = ((), (), s32[]{:S(2)}) async-start(), calls=%async_computation.2 | async-start | bytes 249856 | tf_op jit(solution)/shard_map/psum | solution.py:394
  541.7 53.3 %copy-start.41 = (f32[4,490,1,12,32]{1,4,3,0,2:T(8,128)}, f32[4,490,1,12,32]{1,4,3,0,2:T(8,128)S(1)}, u32[]{:S(2)}) copy-start(f32[4,490,1,12,32]{1,4,3,0,2:T(8,128)S(1)} %convolution_bitcast_fusion.6) | copy-start | bytes 9031684
  606.1 14.5 copy-start.12
  606.1 14.5 copy-start.82
  606.1 14.5 copy-start.108
  638.5 25.5 %collective-permute-start.10 = (bf16[4,1,70,384]{3,2,1,0:T(8,128)(2,1)}, bf16[4,1,70,384]{3,2,1,0:T(8,128)(2,1)}, u32[]{:S(2)}, u32[]{:S(2)}) collective-permute-start(bf16[4,1,70,384]{3,2,1,0:T(8,128)(2,1)} %get-tuple-element.228), channel_id=1, source_target_pairs={{0,1},{1,2},{2,3},{4,5},{5,6},{6,7},{8,9},{9,10},{10,11},{12,13},{... | collective-permute-start | bytes 645128 | tf_op jit(solution)/shard_map/ppermute | solution.py:22
  642.3 21.7 %collective-permute-start.11 = (bf16[4,1,70,384]{3,2,1,0:T(8,128)(2,1)S(1)}, bf16[4,1,70,384]{3,2,1,0:T(8,128)(2,1)}, u32[]{:S(2)}, u32[]{:S(2)}) collective-permute-start(bf16[4,1,70,384]{3,2,1,0:T(8,128)(2,1)S(1)} %get-tuple-element.229), channel_id=1, source_target_pairs={{1,0},{2,1},{3,2},{5,4},{6,5},{7,6},{9,8},{10,9},{11,10},{13,12},{... | collective-permute-start | bytes 645128 | tf_op jit(solution)/shard_map/ppermute | solution.py:24
  679.8 15.1 %copy-start.44 = (bf16[1960,384]{1,0:T(8,128)(2,1)S(1)}, bf16[1960,384]{1,0:T(8,128)(2,1)}, u32[]{:S(2)}) copy-start(bf16[1960,384]{1,0:T(8,128)(2,1)} %reshape.407) | copy-start | bytes 4515844
  721.4 17.1 %collective-permute-start.12 = (bf16[4,1,70,384]{3,2,1,0:T(8,128)(2,1)S(1)}, bf16[4,1,70,384]{3,2,1,0:T(8,128)(2,1)S(1)}, u32[]{:S(2)}, u32[]{:S(2)}) collective-permute-start(bf16[4,1,70,384]{3,2,1,0:T(8,128)(2,1)S(1)} %get-tuple-element.226), channel_id=1, source_target_pairs={{0,1},{1,2},{2,3},{4,5},{5,6},{6,7},{8,9},{9,10},{10,11},{12,13},{... | collective-permute-start | bytes 645128 | tf_op jit(solution)/shard_map/ppermute | solution.py:22
  725.9 12.6 collective-permute-start.13
  1057.2 12.3 copy-start.53
  1068.3 384.9 %all-reduce.21.cloned.1.call-start = ((), (), s32[]{:S(2)}) async-start(), calls=%async_computation.3 | async-start | bytes 28311552 | tf_op jit(solution)/shard_map/psum | solution.py:394
  1069.6 128.7 %collective-permute-start.14 = (bf16[4,1,70,384]{3,2,1,0:T(8,128)(2,1)S(1)}, bf16[4,1,70,384]{3,2,1,0:T(8,128)(2,1)}, u32[]{:S(2)}, u32[]{:S(2)}) collective-permute-start(bf16[4,1,70,384]{3,2,1,0:T(8,128)(2,1)S(1)} %get-tuple-element.224), channel_id=1, source_target_pairs={{0,1},{1,2},{2,3},{4,5},{5,6},{6,7},{8,9},{9,10},{10,11},{12,13},{... | collective-permute-start | bytes 645128 | tf_op jit(solution)/shard_map/ppermute | solution.py:22
  1074.8 123.5 %collective-permute-start.15 = (bf16[4,1,70,384]{3,2,1,0:T(8,128)(2,1)S(1)}, bf16[4,1,70,384]{3,2,1,0:T(8,128)(2,1)}, u32[]{:S(2)}, u32[]{:S(2)}) collective-permute-start(bf16[4,1,70,384]{3,2,1,0:T(8,128)(2,1)S(1)} %get-tuple-element.225), channel_id=1, source_target_pairs={{1,0},{2,1},{3,2},{5,4},{6,5},{7,6},{9,8},{10,9},{11,10},{13,12},{... | collective-permute-start | bytes 645128 | tf_op jit(solution)/shard_map/ppermute | solution.py:24
  1077.8 122.6 %copy-start.24 = (f32[4,7,70,384]{3,2,1,0:T(8,128)S(1)}, f32[4,7,70,384]{3,2,1,0:T(8,128)}, u32[]{:S(2)}) copy-start(f32[4,7,70,384]{3,2,1,0:T(8,128)} %copy-done.23) | copy-start | bytes 9031684
  1077.8 122.6 %copy-start.115 = (f32[384]{0:T(512)S(1)}, f32[384]{0:T(512)}, u32[]{:S(2)}) copy-start(f32[384]{0:T(512)} %copy-done.114) | copy-start | bytes 4612
  1077.8 122.6 %copy-start.117 = (f32[384]{0:T(512)S(1)}, f32[384]{0:T(512)}, u32[]{:S(2)}) copy-start(f32[384]{0:T(512)} %copy-done.116) | copy-start | bytes 4612
  1077.8 122.6 %copy-start.119 = (f32[384]{0:T(512)S(1)}, f32[384]{0:T(512)}, u32[]{:S(2)}) copy-start(f32[384]{0:T(512)} %copy-done.118) | copy-start | bytes 4612
  1204.0 249.2 %copy-start.205 = (f32[4,384]{1,0:T(4,128)S(1)}, f32[4,384]{1,0:T(4,128)}, u32[]{:S(2)}) copy-start(f32[4,384]{1,0:T(4,128)} %get-tuple-element.276) | copy-start | bytes 18436
  1204.0 249.8 %copy-start.204 = (f32[4,384]{1,0:T(4,128)S(1)}, f32[4,384]{1,0:T(4,128)}, u32[]{:S(2)}) copy-start(f32[4,384]{1,0:T(4,128)} %get-tuple-element.277) | copy-start | bytes 18436
  1204.1 250.4 %copy-start.203 = (f32[3,384]{1,0:T(4,128)S(1)}, f32[3,384]{1,0:T(4,128)}, u32[]{:S(2)}) copy-start(f32[3,384]{1,0:T(4,128)} %get-tuple-element.278) | copy-start | bytes 13828
  1204.1 251.0 %copy-start.220 = (f32[384]{0:T(512)S(1)}, f32[384]{0:T(512)}, u32[]{:S(2)}) copy-start(f32[384]{0:T(512)} %get-tuple-element.279) | copy-start | bytes 4612
  (211 other events, 1262.9 us)
Sparse Core Ops, SparseCore 0:
  327.1 41.8 all-reduce.14
  537.4 43.8 all-reduce.16
  1068.4 128.2 all-reduce.18
  1205.3 247.8 all-reduce.20
where the time goes:
time: 1490 us; the launch traced here: 1480 us
  local copies, waits for them, and re-layouts  496 us (33%)
  waiting for transfers between devices  466 us (31%)
  matrix products  280 us (19%)
  other arithmetic  172 us (12%)
  starting transfers between devices  44.7 us (3%)
  between operations  17.5 us (1%)
    psum x2, waiting for transfers between devices, local(): lax.psum((conv_w_grad, conv_b_grad, gain_grad, shift_grad, final_shift, m...  366 us
    reshape x5, local copies, waits for them, and re-layouts, from_windows(): windows.reshape(images, height // 7, width // 7, HEADS, 7, 7, HEAD_DIM)  73.5 us
    dot_general x2, matrix products, mlp_forward(): pre_act = jnp.dot(normed, up_w, preferred_element_type=jnp.float32) + up_b  62.1 us
    reshape x4, local copies, waits for them, and re-layouts, to_windows(): blocks.transpose(0, 1, 3, 5, 2, 4, 6).reshape(-1, HEADS, 49, HEAD_DIM)  45.4 us
    unnamed x496, local copies, waits for them, and re-layouts  42.9 us
    another operation x5, local copies, waits for them, and re-layouts  42.6 us
    psum x1, waiting for transfers between devices, channel_forward(): gram = lax.psum(partial_gram, 'rows')  41.9 us
    reshape x4, local copies, waits for them, and re-layouts, from_windows(): blocks.transpose(0, 1, 4, 2, 5, 3, 6)  40.2 us
  transfers between devices with their start and end apart: 20, of which 11 were waited for; matrix products, arithmetic and copies ran while one was open for 4% of the time, Pallas kernels for 0%

commit v1 on v0

v1 whole, which is shorter than its diff:
```python
import functools

import jax
import jax.numpy as jnp
from jax import lax
from jax.experimental import pallas as pl
from jax.experimental.pallas import tpu as pltpu
from jax.sharding import Mesh
from jax.sharding import PartitionSpec as P

HEADS = 12
HEAD_DIM = 32
EPS = 1e-05
WIN = 7
SLOT = 64
LANES = 128
F32 = jnp.float32
BF16 = jnp.bfloat16
SCALE = HEAD_DIM ** (-0.5)
LOG2E = 1.4426950408889634
ROOT_HALF = 0.7071067811865476
VMEM_LIMIT = 58 * 1024 * 1024
SMALL_ROWS = 256


def dot(left, right):
    return jnp.dot(left, right, preferred_element_type=F32)


def dot_nt(left, right):
    return lax.dot_general(left, right, (((1,), (1,)), ((), ())), preferred_element_type=F32)


def dot_tn(left, right):
    return lax.dot_general(left, right, (((0,), (0,)), ((), ())), preferred_element_type=F32)


def low(value):
    return value.astype(BF16).astype(F32)


def fold(value):
    rows, cols = value.shape
    return jnp.sum(value.reshape(rows // 8, 8, cols), axis=0)


def loop(count, step, body):
    for at in range(0, count, step):
        body(at)


def lane_tiles(chans):
    return [slice(t, t + LANES) for t in range(0, chans, LANES)]


def gelu_parts(value):
    size = jnp.abs(value)
    t = 1.0 / (1.0 + (0.3275911 * ROOT_HALF) * size)
    poly = t * (
        0.127414796
        + t * (-0.142248368 + t * (0.7107068705 + t * (-0.7265760135 + t * 0.5307027145)))
    )
    bell = jnp.exp2(value * value * (-0.5 * LOG2E))
    tail = poly * bell
    cdf = jnp.where(value >= 0.0, 1.0 - tail, tail)
    return value * cdf, cdf + value * bell * 0.3989422804014327


def norm_of(value, gain, shift):
    centre = value - jnp.mean(value, axis=-1, keepdims=True)
    spread = jnp.mean(centre * centre, axis=-1, keepdims=True)
    return centre * lax.rsqrt(spread + EPS) * gain + shift


def norm_back(value, gain, normed_grad):
    centre = value - jnp.mean(value, axis=-1, keepdims=True)
    inv = lax.rsqrt(jnp.mean(centre * centre, axis=-1, keepdims=True) + EPS)
    unit = centre * inv
    unit_grad = normed_grad * gain
    first = jnp.mean(unit_grad, axis=-1, keepdims=True)
    second = jnp.mean(unit_grad * unit, axis=-1, keepdims=True)
    return inv * (unit_grad - first - unit * second), normed_grad * unit


def fill_source(src, main, prev, after, halo, step, steps, width):
    rows = main.shape[0]
    src[pl.ds(0, width), :] = jnp.where(step == 0, halo[0:width, :], low(prev[...]))
    src[pl.ds(rows + width, width), :] = jnp.where(
        step == steps - 1, halo[width : 2 * width, :], low(after[...])
    )

    def body(at):
        src[pl.ds(at + width, 2 * width), :] = low(main[pl.ds(at, 2 * width), :])

    loop(rows // (2 * width) * 2 * width, 2 * width, body)
    if rows % (2 * width):
        at = rows - width
        src[pl.ds(at + width, width), :] = low(main[pl.ds(at, width), :])


def conv_tile(src, vec, at, tile, width, lanes, flipped):
    rows = [src[pl.ds(at + width * d, tile), lanes] for d in range(3)]
    sums = []
    for col in range(3):
        total = None
        for row in range(3):
            k = (2 - row) * 3 + (2 - col) if flipped else row * 3 + col
            term = rows[row] * vec[k : k + 1, lanes]
            total = term if total is None else total + term
        sums.append(total)
    return sums[1] + pltpu.roll(sums[0], 1, 0) + pltpu.roll(sums[2], tile - 1, 0), rows


def conv_weight_tile(acc, rows, field, tile, lanes):
    shifted = [pltpu.roll(field, 1, 0), field, pltpu.roll(field, tile - 1, 0)]
    for row in range(3):
        for col in range(3):
            k = row * 3 + col
            acc[8 * k : 8 * k + 8, lanes] += fold(shifted[col] * rows[2 - row])


def block_heads(part):
    lane = lax.broadcasted_iota(jnp.int32, part.shape, 1)
    zero = jnp.zeros_like(part)
    return jnp.concatenate(
        [jnp.where(lane // HEAD_DIM == h, part, zero) for h in range(LANES // HEAD_DIM)], axis=0
    )


def window_forward_kernel(
    tok, prev, after, halo, mask, vec, mix, mix_b, out_w, gather, x1, nw, mw, ow, x2, src, keep, probs
):
    step, steps = pl.program_id(0), pl.num_programs(0)
    rows, width, chans = tok.shape
    src[pl.ds(0, width), :] = jnp.where(step == 0, halo[0:width, :], prev[0].astype(F32))
    src[pl.ds((rows + 1) * width, width), :] = jnp.where(
        step == steps - 1, halo[width : 2 * width, :], after[0].astype(F32)
    )
    for i in range(rows):
        src[pl.ds((i + 1) * width, width), :] = tok[i].astype(F32)

    def conv_body(at):
        region = mask[pl.ds(at, width), :]
        for lanes in lane_tiles(chans):
            got, near = conv_tile(src, vec, at, width, width, lanes, False)
            x1[pl.ds(at, width), lanes] = region * (near[1] + got + vec[9:10, lanes])

    loop(rows * width, width, conv_body)

    normed = norm_of(x1[...], vec[10:11, :], vec[11:12, :]).astype(BF16)
    normed = dot(gather[...], normed).astype(BF16)
    nw[...] = normed
    mw[...] = (dot(normed, mix[...]) + mix_b[...]).astype(BF16)
    windows = nw.shape[0] // SLOT
    lane = lax.broadcasted_iota(jnp.int32, (SLOT, LANES), 1)
    left = lane < SLOT
    real = lane % SLOT < WIN * WIN
    ones = (
        lax.broadcasted_iota(jnp.int32, (4 * SLOT, LANES), 0) // SLOT
        == lax.broadcasted_iota(jnp.int32, (4 * SLOT, LANES), 1) // HEAD_DIM
    ).astype(BF16)
    floor = -1e30

    places = [(at, lanes) for at in range(0, windows * SLOT, SLOT) for lanes in lane_tiles(chans)]
    for n, (at, lanes) in enumerate(places):
        query = mw[at : at + SLOT, lanes]
        key = mw[at : at + SLOT, chans + lanes.start : chans + lanes.stop]
        scores = dot_nt(query, block_heads(key))
        for half in range(2):
            part = jnp.where(real, scores[:, half * LANES : (half + 1) * LANES], floor)
            top_l = jnp.max(jnp.where(left, part, floor), axis=1, keepdims=True)
            top_r = jnp.max(jnp.where(left, floor, part), axis=1, keepdims=True)
            top = jnp.where(left, top_l, top_r)
            raised = jnp.exp2((part - top) * (SCALE * LOG2E)).astype(BF16)
            probs[n * SLOT : (n + 1) * SLOT, half * LANES : (half + 1) * LANES] = raised
    for n, (at, lanes) in enumerate(places):
        value = mw[at : at + SLOT, 2 * chans + lanes.start : 2 * chans + lanes.stop]
        both = dot(
            probs[n * SLOT : (n + 1) * SLOT, :], jnp.concatenate([block_heads(value), ones], axis=1)
        )
        ow[at : at + SLOT, lanes] = (both[:, :LANES] / both[:, LANES:]).astype(BF16)
    merged = dot_tn(gather[...], ow[...]).astype(BF16)
    keep[...] = dot(merged, out_w[...])

    def out_body(at):
        region = mask[pl.ds(at, width), :]
        for lanes in lane_tiles(chans):
            x2[pl.ds(at, width), lanes] = region * (
                x1[pl.ds(at, width), lanes] + keep[pl.ds(at, width), lanes] + vec[12:13, lanes]
            )

    loop(rows * width, width, out_body)


def conv_forward(main, prev, after, halo, mask, vec, out, src, width):
    step, steps = pl.program_id(0), pl.num_programs(0)
    rows, chans = main.shape
    fill_source(src, main, prev, after, halo, step, steps, width)
    tile = 2 * width

    def body(at):
        region = mask[pl.ds(at, tile), :]
        for lanes in lane_tiles(chans):
            got, _ = conv_tile(src, vec, at, tile, width, lanes, False)
            out[pl.ds(at, tile), lanes] = region * (
                main[pl.ds(at, tile), lanes] + got + vec[9:10, lanes]
            )

    loop(rows, tile, body)


def norm_forward(value, vec, out):
    out[...] = norm_of(value[...], vec[10:11, :], vec[11:12, :]).astype(BF16)


def mlp_body(normed, up_w, up_b, down_w, hidden, slope, keep):
    rows = normed.shape[0]
    for at in range(0, up_w.shape[1], 256):
        cols = slice(at, at + 256)
        pre = dot(normed[...], up_w[:, cols]) + up_b[:, cols]
        for row in range(0, rows, 144):
            act, der = gelu_parts(pre[row : row + 144])
            hidden[row : row + 144, cols] = act.astype(BF16)
            slope[row : row + 144, cols] = der.astype(BF16)
        part = dot(hidden[:, cols], down_w[cols, :])
        if at == 0:
            keep[...] = part
        else:
            keep[...] += part


def add_residual(state, branch, mask, vec, out):
    chans = state.shape[1]

    def body(at):
        region = mask[pl.ds(at, 144), :]
        for lanes in lane_tiles(chans):
            out[pl.ds(at, 144), lanes] = (
                region
                * (state[pl.ds(at, 144), lanes] + branch[pl.ds(at, 144), lanes] + vec[12:13, lanes])
            ).astype(out.dtype)

    loop(state.shape[0], 144, body)


def mlp_forward_kernel(
    main, prev, after, halo, mask, vec, up_w, up_b, down_w, x3, x4, normed, hidden, slope, src, keep
):
    width = prev.shape[0]
    conv_forward(main, prev, after, halo, mask, vec, x3, src, width)
    norm_forward(x3, vec, normed)
    mlp_body(normed, up_w, up_b, down_w, hidden, slope, keep)
    add_residual(x3, keep, mask, vec, x4)


def norm_backward(state, normed_grad, grad, vec, small, out, gain_row):
    part = normed_grad[...]
    back, scaled = norm_back(state[...], vec[10:11, :], part)
    out[...] = grad[...].astype(F32) + back
    small[gain_row : gain_row + 8, :] += fold(scaled)
    small[gain_row + 8 : gain_row + 16, :] += fold(part)


def mlp_down_back(rounded, normed, hidden, slope, pre_grad, up_w, down_w, up_g, up_bg, down_g):
    rows = rounded.shape[0]
    for at in range(0, up_w.shape[1], 256):
        cols = slice(at, at + 256)
        hidden_grad = dot_nt(rounded[...], down_w[cols, :])
        total = None
        for row in range(0, rows, 144):
            part = hidden_grad[row : row + 144] * slope[row : row + 144, cols].astype(F32)
            pre_grad[row : row + 144, cols] = part.astype(BF16)
            total = fold(part) if total is None else total + fold(part)
        up_bg[:, cols] += total
        up_g[:, cols] += dot_tn(normed[...], pre_grad[:, cols])
        down_g[cols, :] += dot_tn(hidden[:, cols], rounded[...])


def mlp_both(normed, cot, up_w, up_b, down_w, hidden, pre_grad, up_g, up_bg, down_g):
    rows = normed.shape[0]
    for at in range(0, up_w.shape[1], 256):
        cols = slice(at, at + 256)
        pre = dot(normed[...], up_w[:, cols]) + up_b[:, cols]
        hidden_grad = dot_nt(cot[...], down_w[cols, :])
        total = None
        for row in range(0, rows, 144):
            act, der = gelu_parts(pre[row : row + 144])
            hidden[row : row + 144, cols] = act.astype(BF16)
            part = hidden_grad[row : row + 144] * der
            pre_grad[row : row + 144, cols] = part.astype(BF16)
            total = fold(part) if total is None else total + fold(part)
        up_bg[:, cols] += total
        up_g[:, cols] += dot_tn(normed[...], pre_grad[:, cols])
        down_g[cols, :] += dot_tn(hidden[:, cols], cot[...])


def column_blocks(source, chans):
    return [source.at[:, col : col + chans] for col in range(0, source.shape[1], chans)]


def spread(core, kept, sent, blocks):
    half = kept.shape[0]
    for flag in range(2):

        @pl.when(core[0] == flag)
        def _():
            at = 0
            for block in blocks:
                rows = block.shape[0]
                cuts = [0, rows] if not at < half < at + rows else [0, half - at, rows]
                for low_cut, high_cut in zip(cuts, cuts[1:]):
                    start = at + low_cut
                    target = kept if (start >= half) == (flag == 1) else sent
                    start = start % half
                    target[start : start + high_cut - low_cut, :] = block[
                        low_cut:high_cut, :
                    ].astype(BF16)
                at += rows


def last_step():
    return pl.program_id(0) == pl.num_programs(0) - 1


def zero_first(*refs):
    @pl.when(pl.program_id(0) == 0)
    def _():
        for ref in refs:
            ref[...] = jnp.zeros_like(ref)


def last_mlp_kernel(
    main, prev, after, halo, mask, vec, up_w, up_b, down_w, cot,
    result, grad, packed, up_bg, small,
    src, x7, keep, back, normed, hidden, pre_grad, up_g, down_g,
):
    width = prev.shape[0]
    zero_first(up_g, up_bg, down_g, small)
    conv_forward(main, prev, after, halo, mask, vec, x7, src, width)
    norm_forward(x7, vec, normed)
    mlp_both(normed, cot, up_w, up_b, down_w, hidden, pre_grad, up_g, up_bg, down_g)
    keep[...] = dot(hidden[...], down_w[...])
    back[...] = dot_nt(pre_grad[...], up_w[...])
    add_residual(x7, keep, mask, vec, result)
    small[0:8, :] += fold(cot[...].astype(F32))
    norm_backward(x7, back, cot, vec, small, grad, 8)

    @pl.when(last_step())
    def _():
        at = 0
        for block in column_blocks(up_g, packed.shape[1]) + [down_g]:
            packed[at : at + block.shape[0], :] = block[...].astype(BF16)
            at += block.shape[0]


def conv_backward(main, prev, after, halo, mask, vec, field, out, conv_g, small, src, width):
    step, steps = pl.program_id(0), pl.num_programs(0)
    rows, chans = main.shape
    fill_source(src, main, prev, after, halo, step, steps, width)
    tile = 72

    def body(at):
        region = mask[pl.ds(at, tile), :]
        for lanes in lane_tiles(chans):
            got, near = conv_tile(src, vec, at, tile, width, lanes, True)
            grad = main[pl.ds(at, tile), lanes]
            out[pl.ds(at, tile), lanes] = (region * (grad + got)).astype(out.dtype)
            conv_weight_tile(conv_g, near, low(field[pl.ds(at, tile), lanes]), tile, lanes)
            small[0:8, lanes] += fold(grad)

    loop(rows, tile, body)


def fold_rows(source, small, row):
    def body(at):
        small[row : row + 8, :] += fold(source[pl.ds(at, 72), :])

    loop(source.shape[0], 72, body)


def channel_mix_kernel(
    main, prev, after, halo, mask, vec, mix, mix_b, x5, normed, mixed, gram, src
):
    width = prev.shape[0]
    chans = main.shape[1]
    zero_first(gram)
    conv_forward(main, prev, after, halo, mask, vec, x5, src, width)
    norm_forward(x5, vec, normed)
    rows = main.shape[0]
    for part in range(3):
        cols = slice(part * chans, (part + 1) * chans)
        got = dot(normed[...], mix[:, cols]) + mix_b[:, cols]
        if part == 1:
            got = got * jnp.concatenate([mask[...]] * (chans // LANES), axis=1)
        mixed[:, cols] = got.astype(BF16)
    for t, lanes in enumerate(lane_tiles(chans)):
        gram[t] += dot_tn(
            mixed[:, chans + lanes.start : chans + lanes.stop],
            mixed[:, 2 * chans + lanes.start : 2 * chans + lanes.stop],
        )


def same_head():
    row = lax.broadcasted_iota(jnp.int32, (LANES, LANES), 0)
    col = lax.broadcasted_iota(jnp.int32, (LANES, LANES), 1)
    return row // HEAD_DIM == col // HEAD_DIM


def channel_weights(gram, scale):
    own = same_head()
    logits = jnp.where(own, gram * scale, -1e30)
    top = jnp.max(logits, axis=1, keepdims=True)
    raised = jnp.where(own, jnp.exp(logits - top), 0.0)
    return raised / jnp.sum(raised, axis=1, keepdims=True)


def channel_out_kernel(mixed, gram, scale, x5, mask, vec, out_w, o2, x6, keep):
    chans = x5.shape[1]
    for t, lanes in enumerate(lane_tiles(chans)):
        weights = channel_weights(gram[t], scale[0:1, :]).astype(BF16)
        o2[:, lanes] = dot_nt(mixed[:, lanes], weights).astype(BF16)
    keep[...] = dot(o2[...], out_w[...])
    add_residual(x5, keep, mask, vec, x6)


def channel_grad_kernel(
    main, prev, after, halo, mask, vec, x6, mixed, o2, out_w,
    grad, attended_grad, weights_g, packed, conv_g, small, src, rounded, out_g,
):
    width = prev.shape[0]
    chans = main.shape[1]
    zero_first(weights_g, out_g, conv_g, small)
    conv_backward(main, prev, after, halo, mask, vec, x6, grad, conv_g, small, src, width)
    rounded[...] = grad[...].astype(BF16)
    fold_rows(grad, small, 8)
    out_g[...] += dot_tn(o2[...], rounded[...])
    attended_grad[...] = dot_nt(rounded[...], out_w[...]).astype(BF16)
    for t, lanes in enumerate(lane_tiles(chans)):
        weights_g[t] += dot_tn(attended_grad[:, lanes], mixed[:, lanes])

    @pl.when(last_step())
    def _():
        packed[...] = out_g[...].astype(BF16)


def channel_back_kernel(
    attended_grad, mixed, gram, weights_g, scale, normed, x5, g6, mask, vec, mix,
    grad, packed, mix_bg, small, mixed_grad, keep, mix_g,
):
    chans = x5.shape[1]
    zero_first(mix_g, mix_bg, small)
    own = same_head()
    wide = mask[...]
    for t, lanes in enumerate(lane_tiles(chans)):
        weights = channel_weights(gram[t], scale[0:1, :])
        back = jnp.where(own, weights_g[t], 0.0)
        logit = weights * (back - jnp.sum(back * weights, axis=1, keepdims=True))
        logit = logit.astype(BF16)
        key = slice(chans + lanes.start, chans + lanes.stop)
        val = slice(2 * chans + lanes.start, 2 * chans + lanes.stop)
        query_grad = dot(attended_grad[:, lanes], weights.astype(BF16))
        key_grad = dot_nt(mixed[:, val], logit) * scale[0:1, :] * wide
        value_grad = dot(mixed[:, key], logit) * scale[0:1, :]
        for cols, part in ((lanes, query_grad), (key, key_grad), (val, value_grad)):
            mix_bg[:, cols] += fold(part)
            mixed_grad[:, cols] = part.astype(BF16)
    for part in range(3):
        cols = slice(part * chans, (part + 1) * chans)
        mix_g[part * chans : (part + 1) * chans, :] += dot_tn(normed[...], mixed_grad[:, cols])
    keep[...] = dot_nt(mixed_grad[...], mix[...])
    norm_backward(x5, keep, g6, vec, small, grad, 0)

    @pl.when(last_step())
    def _():
        packed[...] = mix_g[...].astype(BF16)


def mlp_back_kernel(
    main, prev, after, halo, mask, vec_conv, vec, x4, x3, normed, hidden, slope, up_w, down_w, mlp1, mix1, out1, core,
    grad, kept, sent, up_bg, conv_g, small,
    src, g4, rounded, keep, pre_grad, up_g, down_g,
):
    width = prev.shape[0]
    zero_first(up_g, up_bg, down_g, conv_g, small)
    conv_backward(main, prev, after, halo, mask, vec_conv, x4, g4, conv_g, small, src, width)
    rounded[...] = g4[...].astype(BF16)
    fold_rows(g4, small, 8)
    mlp_down_back(rounded, normed, hidden, slope, pre_grad, up_w, down_w, up_g, up_bg, down_g)
    keep[...] = dot_nt(pre_grad[...], up_w[...])
    norm_backward(x3, keep, g4, vec, small, grad, 16)

    @pl.when(last_step())
    def _():
        spread(core, kept, sent, [mlp1, mix1, out1] + column_blocks(up_g, kept.shape[1]) + [down_g])


def window_back_kernel(
    main, prev, after, halo, mask, vec_conv, vec, x2, x1, nw, mw, ow, mix, out_w, gather,
    grad, packed, mix_bg, conv_g, small,
    src, mix_g, out_g, g2, gw, dow, dmw, keep, probs, slopes,
):
    width = prev.shape[0]
    chans = main.shape[1]
    zero_first(mix_g, mix_bg, out_g, conv_g, small)
    conv_backward(main, prev, after, halo, mask, vec_conv, x2, g2, conv_g, small, src, width)
    fold_rows(g2, small, 8)
    gw[...] = dot(gather[...], g2[...].astype(BF16)).astype(BF16)
    out_g[...] += dot_tn(ow[...], gw[...])
    dow[...] = dot_nt(gw[...], out_w[...]).astype(BF16)
    windows = nw.shape[0] // SLOT
    real = lax.broadcasted_iota(jnp.int32, (SLOT, 4 * SLOT), 0) < WIN * WIN
    head = lax.broadcasted_iota(jnp.int32, (SLOT, LANES), 1) // HEAD_DIM

    places = [(at, lanes) for at in range(0, windows * SLOT, SLOT) for lanes in lane_tiles(chans)]
    for n, (at, lanes) in enumerate(places):
        rows = slice(at, at + SLOT)
        query = mw[rows, lanes]
        key = mw[rows, chans + lanes.start : chans + lanes.stop]
        value = mw[rows, 2 * chans + lanes.start : 2 * chans + lanes.stop]
        scores = jnp.where(real, dot_nt(key, block_heads(query)), -1e30)
        top = jnp.max(scores, axis=0, keepdims=True)
        raised = jnp.exp2((scores - top) * (SCALE * LOG2E))
        share = raised * (1.0 / jnp.sum(raised, axis=0, keepdims=True))
        share_grad = dot_nt(value, block_heads(dow[rows, lanes]))
        inner = jnp.sum(share_grad * share, axis=0, keepdims=True)
        probs[n * SLOT : (n + 1) * SLOT, :] = share.astype(BF16)
        slopes[n * SLOT : (n + 1) * SLOT, :] = (share * (share_grad - inner)).astype(BF16)
    for n, (at, lanes) in enumerate(places):
        rows = slice(at, at + SLOT)
        key_cols = slice(chans + lanes.start, chans + lanes.stop)
        value_cols = slice(2 * chans + lanes.start, 2 * chans + lanes.stop)
        share, slope = probs[n * SLOT : (n + 1) * SLOT, :], slopes[n * SLOT : (n + 1) * SLOT, :]
        value_grad = dot(share, block_heads(dow[rows, lanes]))
        key_grad = dot(slope, block_heads(mw[rows, lanes])) * SCALE
        full = dot_tn(slope, mw[rows, key_cols])
        query_grad = jnp.zeros((SLOT, LANES), F32)
        for h in range(LANES // HEAD_DIM):
            query_grad = jnp.where(head == h, full[h * SLOT : (h + 1) * SLOT], query_grad)
        query_grad = query_grad * SCALE
        for cols, part in ((lanes, query_grad), (key_cols, key_grad), (value_cols, value_grad)):
            dmw[rows, cols] = part.astype(BF16)
            mix_bg[:, cols] += fold(part)
    for part in range(3):
        cols = slice(part * chans, (part + 1) * chans)
        mix_g[part * chans : (part + 1) * chans, :] += dot_tn(nw[...], dmw[:, cols])
    normed_grad = dot_nt(dmw[...], mix[...]).astype(BF16)
    keep[...] = dot_tn(gather[...], normed_grad)
    norm_backward(x1, keep, g2, vec, small, grad, 16)

    @pl.when(last_step())
    def _():
        packed[: 3 * chans, :] = mix_g[...].astype(BF16)
        packed[3 * chans :, :] = out_g[...].astype(BF16)


def token_grad_kernel(main, prev, after, halo, mask, vec, field, out, conv_g, small, src):
    width = prev.shape[0]
    zero_first(conv_g, small)
    conv_backward(main, prev, after, halo, mask, vec, field, out, conv_g, small, src, width)


def call(kernel, steps, ins, outs, scratch, cost, after=()):
    count = len(ins)

    def body(*refs):
        kernel(*refs[:count], *refs[count + len(after) :])

    def spec(block, index):
        if block is None:
            return pl.BlockSpec(memory_space=pltpu.SMEM)
        fixed = tuple(0 for _ in block)
        if index is None:
            return pl.BlockSpec(block, lambda i: fixed, pipeline_mode=pl.Buffered(1))
        return pl.BlockSpec(block, index)

    def out_spec(block, index):
        fixed = tuple(0 for _ in block)
        return pl.BlockSpec(block, (lambda i: fixed) if index is None else index)

    return pl.pallas_call(
        body,
        grid=(steps,),
        in_specs=[spec(block, index) for _, block, index in ins]
        + [pl.BlockSpec(memory_space=pl.ANY) for _ in after],
        out_specs=[out_spec(block, index) for _, _, block, index in outs],
        out_shape=[jax.ShapeDtypeStruct(shape, dtype) for shape, dtype, _, _ in outs],
        scratch_shapes=[pltpu.VMEM(shape, dtype) for shape, dtype in scratch],
        compiler_params=pltpu.CompilerParams(vmem_limit_bytes=VMEM_LIMIT),
        cost_estimate=pl.CostEstimate(flops=1, bytes_accessed=1, transcendentals=0),
    )(*[array for array, _, _ in ins], *after)


def gather_matrix(cols, width):
    windows = cols // WIN
    slot = jnp.arange(windows * SLOT, dtype=jnp.int32)[:, None]
    window, inside = slot // SLOT, slot % SLOT
    source = inside // WIN * width + window * WIN + inside % WIN
    patch = jnp.arange(WIN * width, dtype=jnp.int32)[None, :]
    return ((source == patch) & (inside < WIN * WIN)).astype(BF16)


def image_block(x0, cot, tok_halo, mask, scale, halo_of, across, weights, cols, core, send_result, share_cores, share_planes):
    conv_w, conv_b, gain, shift, mix_w, win_b, chan_b, out_w, out_b, up_w, up_b, down_w, down_b = weights
    height, width, chans = x0.shape
    tokens = height * width
    ff = up_w.shape[2]
    vec_of = [
        jnp.concatenate(
            [
                conv_w[k].reshape(9, chans),
                conv_b[k : k + 1],
                gain[k : k + 1],
                shift[k : k + 1],
                (out_b if k % 2 == 0 else down_b)[k // 2 : k // 2 + 1],
                jnp.zeros((3, chans), BF16),
            ],
            axis=0,
        ).astype(F32)
        for k in range(4)
    ]
    bias0 = jnp.concatenate([win_b[:chans], jnp.zeros((chans,), BF16), win_b[chans:]])
    bias0 = bias0.astype(F32)[None]
    bias1 = chan_b.astype(F32)[None]
    up_bias = up_b.astype(F32)
    gather = gather_matrix(cols, width)
    wrows = cols // WIN * SLOT
    unit = WIN * width
    units = height // WIN
    chunk = 2 * unit if units % 2 == 0 else unit
    chunks = tokens // chunk

    def near(array, rows):
        per = rows // width
        return [
            (array, (rows, chans), lambda i: (i, 0)),
            (array, (width, chans), lambda i: (jnp.maximum(i * per - 1, 0), 0)),
            (array, (width, chans), lambda i: (jnp.minimum(i * per + per, height - 1), 0)),
            (halo_of(array), (2 * width, chans), None),
        ]

    def rows_in(array, rows):
        return (array, (rows, array.shape[1]), lambda i: (i, 0))

    def whole(array):
        return (array, array.shape, None)

    def rows_out(cols_, dtype, rows=chunk, total=tokens):
        return ((total, cols_), dtype, (rows, cols_), lambda i: (i, 0))

    def sums(*shape, dtype=F32):
        return (shape, dtype, shape, None)

    def vec(k):
        return whole(vec_of[k])

    scalar = (core, None, None)

    dense = 2 * tokens * chans
    x1, nw, mw, ow, x2 = call(
        window_forward_kernel,
        units,
        [
            (x0, (WIN, width, chans), lambda i: (i, 0, 0)),
            (x0, (1, width, chans), lambda i: (jnp.maximum(i * WIN - 1, 0), 0, 0)),
            (x0, (1, width, chans), lambda i: (jnp.minimum(i * WIN + WIN, height - 1), 0, 0)),
            whole(tok_halo),
            rows_in(mask, unit),
            vec(0),
            whole(mix_w[0]),
            whole(bias0),
            whole(out_w[0]),
            whole(gather),
        ],
        [
            rows_out(chans, F32, unit),
            rows_out(chans, BF16, wrows, units * wrows),
            rows_out(3 * chans, BF16, wrows, units * wrows),
            rows_out(chans, BF16, wrows, units * wrows),
            rows_out(chans, F32, unit),
        ],
        [
            ((unit + 2 * width, chans), F32),
            ((unit, chans), F32),
            ((wrows * chans // LANES, 4 * SLOT), BF16),
        ],
        dense * 4 * chans,
    )
    x3, x4, n1, h1, s1 = call(
        mlp_forward_kernel,
        chunks,
        near(x2, chunk) + [rows_in(mask, chunk), vec(1), whole(up_w[0]), whole(up_bias[0:1]), whole(down_w[0])],
        [
            rows_out(chans, F32),
            rows_out(chans, F32),
            rows_out(chans, BF16),
            rows_out(ff, BF16),
            rows_out(ff, BF16),
        ],
        [((chunk + 2 * width, chans), F32), ((chunk, chans), F32)],
        dense * 2 * ff,
    )
    x5, n2, m2, gram = call(
        channel_mix_kernel,
        chunks,
        near(x4, chunk) + [rows_in(mask, chunk), vec(2), whole(mix_w[1]), whole(bias1)],
        [
            rows_out(chans, F32),
            rows_out(chans, BF16),
            rows_out(3 * chans, BF16),
            sums(chans // LANES, LANES, LANES),
        ],
        [((chunk + 2 * width, chans), F32)],
        dense * 3 * chans,
    )
    gram = across(gram)
    o2, x6 = call(
        channel_out_kernel,
        chunks,
        [
            rows_in(m2, chunk),
            whole(gram),
            whole(scale),
            rows_in(x5, chunk),
            rows_in(mask, chunk),
            vec(2),
            whole(out_w[1]),
        ],
        [rows_out(chans, BF16), rows_out(chans, F32)],
        [((chunk, chans), F32)],
        dense * 2 * chans,
    )
    result, g7, mlp1, up_bg1, small7 = call(
        last_mlp_kernel,
        chunks,
        near(x6, chunk)
        + [
            rows_in(mask, chunk),
            vec(3),
            whole(up_w[1]),
            whole(up_bias[1:2]),
            whole(down_w[1]),
            rows_in(cot, chunk),
        ],
        [
            rows_out(chans, BF16),
            rows_out(chans, F32),
            sums(2 * ff, chans, dtype=BF16),
            sums(8, ff),
            sums(24, chans),
        ],
        [
            ((chunk + 2 * width, chans), F32),
            ((chunk, chans), F32),
            ((chunk, chans), F32),
            ((chunk, chans), F32),
            ((chunk, chans), BF16),
            ((chunk, ff), BF16),
            ((chunk, ff), BF16),
            ((chans, ff), F32),
            ((ff, chans), F32),
        ],
        dense * 6 * ff,
    )
    result = send_result(result)
    g6, do2, weights_g, out1, conv_g3, small6 = call(
        channel_grad_kernel,
        chunks,
        near(g7, chunk)
        + [
            rows_in(mask, chunk),
            vec(3),
            rows_in(x6, chunk),
            (m2, (chunk, chans), lambda i: (i, 0)),
            rows_in(o2, chunk),
            whole(out_w[1]),
        ],
        [
            rows_out(chans, F32),
            rows_out(chans, BF16),
            sums(chans // LANES, LANES, LANES),
            sums(chans, chans, dtype=BF16),
            sums(72, chans),
            sums(16, chans),
        ],
        [((chunk + 2 * width, chans), F32), ((chunk, chans), BF16), ((chans, chans), F32)],
        dense * 3 * chans,
    )
    weights_g = across(weights_g)
    g5, mix1, mix_bg1, small5 = call(
        channel_back_kernel,
        chunks,
        [
            rows_in(do2, chunk),
            rows_in(m2, chunk),
            whole(gram),
            whole(weights_g),
            whole(scale),
            rows_in(n2, chunk),
            rows_in(x5, chunk),
            rows_in(g6, chunk),
            rows_in(mask, chunk),
            vec(2),
            whole(mix_w[1]),
        ],
        [
            rows_out(chans, F32),
            sums(3 * chans, chans, dtype=BF16),
            sums(8, 3 * chans),
            sums(16, chans),
        ],
        [((chunk, 3 * chans), BF16), ((chunk, chans), F32), ((3 * chans, chans), F32)],
        dense * 7 * chans,
    )
    g3, kept0, sent0, up_bg0, conv_g2, small3 = call(
        mlp_back_kernel,
        chunks,
        near(g5, chunk)
        + [
            rows_in(mask, chunk),
            vec(2),
            vec(1),
            rows_in(x4, chunk),
            rows_in(x3, chunk),
            rows_in(n1, chunk),
            rows_in(h1, chunk),
            rows_in(s1, chunk),
            whole(up_w[0]),
            whole(down_w[0]),
            whole(mlp1),
            whole(mix1),
            whole(out1),
            scalar,
        ],
        [
            rows_out(chans, F32),
            sums(2 * ff + 2 * chans, chans, dtype=BF16),
            sums(2 * ff + 2 * chans, chans, dtype=BF16),
            sums(8, ff),
            sums(72, chans),
            sums(32, chans),
        ],
        [
            ((chunk + 2 * width, chans), F32),
            ((chunk, chans), F32),
            ((chunk, chans), BF16),
            ((chunk, chans), F32),
            ((chunk, ff), BF16),
            ((chans, ff), F32),
            ((ff, chans), F32),
        ],
        dense * 4 * ff,
        after=(result,),
    )
    mid = share_planes(share_cores(kept0, sent0))
    g1, win0, mix_bg0, conv_g1, small1 = call(
        window_back_kernel,
        units,
        near(g3, unit)
        + [
            rows_in(mask, unit),
            vec(1),
            vec(0),
            rows_in(x2, unit),
            rows_in(x1, unit),
            rows_in(nw, wrows),
            rows_in(mw, wrows),
            rows_in(ow, wrows),
            whole(mix_w[0]),
            whole(out_w[0]),
            whole(gather),
        ],
        [
            rows_out(chans, F32, unit),
            sums(4 * chans, chans, dtype=BF16),
            sums(8, 3 * chans),
            sums(72, chans),
            sums(32, chans),
        ],
        [
            ((unit + 2 * width, chans), F32),
            ((3 * chans, chans), F32),
            ((chans, chans), F32),
            ((unit, chans), F32),
            ((wrows, chans), BF16),
            ((wrows, chans), BF16),
            ((wrows, 3 * chans), BF16),
            ((unit, chans), F32),
            ((wrows * chans // LANES, 4 * SLOT), BF16),
            ((wrows * chans // LANES, 4 * SLOT), BF16),
        ],
        dense * 16 * chans,
    )
    x0_flat = x0.reshape(tokens, chans)
    tokens_grad, conv_g0, small0 = call(
        token_grad_kernel,
        chunks,
        near(g1, chunk) + [rows_in(mask, chunk), vec(0), rows_in(x0_flat, chunk)],
        [rows_out(chans, BF16), sums(72, chans), sums(8, chans)],
        [((chunk + 2 * width, chans), F32)],
        dense * 30,
        after=(mid,),
    )

    sums0 = (conv_g0, conv_g1, conv_g2, conv_g3, small0, small1, small3, small5, small6, small7)
    bias_sums = (mix_bg0, mix_bg1, up_bg0, up_bg1)
    kept, sent = fold_small(core, win0, sums0 + bias_sums, chans)
    return result, tokens_grad, mid, kept, sent


def small_kernel(
    core, win0, conv0, conv1, conv2, conv3, s0, s1, s3, s5, s6, s7, mix0, mix1, up0, up1,
    kept, sent, rows,
):
    chans = rows.shape[1]
    rows[...] = jnp.zeros_like(rows)
    place = 0

    def put(part):
        nonlocal place
        rows[place : place + 1, :] = jnp.sum(part, axis=0, keepdims=True)
        place += 1

    for conv in (conv0, conv1, conv2, conv3):
        for k in range(9):
            put(conv[8 * k : 8 * k + 8, :])
    for ref, at in (
        (s0, 0), (s1, 0), (s3, 0), (s6, 0),
        (s1, 16), (s3, 16), (s5, 0), (s7, 8),
        (s1, 24), (s3, 24), (s5, 8), (s7, 16),
        (s1, 8), (s6, 8), (s3, 8), (s7, 0),
    ):
        put(ref[at : at + 8, :])
    for ref in (mix0, mix1, up0, up1):
        for col in range(0, ref.shape[1], chans):
            put(ref[:, col : col + chans])
    spread(core, kept, sent, [win0, rows])


def fold_small(core, win0, parts, chans):
    half = (win0.shape[0] + SMALL_ROWS) // 2
    return pl.pallas_call(
        small_kernel,
        in_specs=[pl.BlockSpec(memory_space=pltpu.SMEM)]
        + [pl.BlockSpec(memory_space=pltpu.VMEM)] * (1 + len(parts)),
        out_shape=[jax.ShapeDtypeStruct((half, chans), BF16)] * 2,
        scratch_shapes=[pltpu.VMEM((SMALL_ROWS, chans), F32)],
        compiler_params=pltpu.CompilerParams(vmem_limit_bytes=VMEM_LIMIT),
    )(core, win0, *parts)


def reader(first, second):
    half = first.shape[0]

    def read(at, count):
        parts = []
        if at < half:
            parts.append(first[at : min(at + count, half), :].astype(F32))
        if at + count > half:
            parts.append(second[max(at - half, 0) : at + count - half, :].astype(F32))
        return parts[0] if len(parts) == 1 else jnp.concatenate(parts, axis=0)

    return read


def put_attention(read, mix_w, out_w):
    chans = out_w.shape[1]
    for k in range(3):
        mix_w[0, :, k * chans : (k + 1) * chans] = read(k * chans, chans)
    out_w[0] = read(3 * chans, chans)


def put_feed(read, at, up_w, down_w):
    chans = down_w.shape[2]
    blocks = up_w.shape[2] // chans
    for k in range(blocks):
        up_w[0, :, k * chans : (k + 1) * chans] = read(at + k * chans, chans)
    for k in range(blocks):
        down_w[0, k * chans : (k + 1) * chans, :] = read(at + (blocks + k) * chans, chans)


def feed_kernel(core, mid_a, mid_b, mix_w, out_w, up_w, down_w):
    layer = pl.program_id(0)
    chans = mid_a.shape[1]
    feed_rows = 2 * up_w.shape[2]
    for flag in range(2):
        mid = reader(*((mid_a, mid_b) if flag == 0 else (mid_b, mid_a)))

        @pl.when((core[0] == flag) & (layer == 0))
        def _():
            put_feed(mid, feed_rows + 4 * chans, up_w, down_w)

        @pl.when((core[0] == flag) & (layer == 1))
        def _():
            put_attention(lambda at, count: mid(feed_rows + at, count), mix_w, out_w)
            put_feed(mid, 0, up_w, down_w)


def late_kernel(
    core, late_a, late_b, mix_in, out_in,
    mix_w, out_w, conv_w, conv_b, gain, shift, last_shift, win_b, chan_b, out_b, up_b, down_b,
    rows,
):
    chans = late_a.shape[1]
    blocks = up_b.shape[1] // chans
    for flag in range(2):
        late = reader(*((late_a, late_b) if flag == 0 else (late_b, late_a)))

        @pl.when(core[0] == flag)
        def _():
            put_attention(late, mix_w, out_w)
            rows[...] = late(4 * chans, SMALL_ROWS)

    at = 0
    for k in range(4):
        for i in range(3):
            conv_w[k, i] = rows[at : at + 3, :]
            at += 3
    for ref in (conv_b, gain):
        ref[...] = rows[at : at + 4, :]
        at += 4
    shift[...] = rows[at : at + 3, :]
    last_shift[...] = rows[at + 3 : at + 4, :]
    at += 4
    for ref in (out_b, down_b):
        ref[...] = rows[at : at + 2, :]
        at += 2
    win_b[0:1, :] = rows[at : at + 1, :]
    win_b[1:2, :] = rows[at + 2 : at + 3, :]
    chan_b[...] = rows[at + 3 : at + 6, :]
    at += 6
    for k in range(2):
        for i in range(blocks):
            up_b[k : k + 1, i * chans : (i + 1) * chans] = rows[at : at + 1, :]
            at += 1


def feed_grads(core, mid, chans, ff):
    mix_shape, out_shape = (2, chans, 3 * chans), (2, chans, chans)
    up_shape, down_shape = (2, chans, ff), (2, ff, chans)
    return pl.pallas_call(
        feed_kernel,
        grid=(2,),
        in_specs=[pl.BlockSpec(memory_space=pltpu.SMEM)]
        + [pl.BlockSpec(x.shape, lambda i: (0, 0), pipeline_mode=pl.Buffered(1)) for x in mid],
        out_specs=[pl.BlockSpec((1,) + x[1:], lambda i: (1, 0, 0)) for x in (mix_shape, out_shape)]
        + [pl.BlockSpec((1,) + x[1:], lambda i: (i, 0, 0)) for x in (up_shape, down_shape)],
        out_shape=[jax.ShapeDtypeStruct(x, F32) for x in (mix_shape, out_shape, up_shape, down_shape)],
        compiler_params=pltpu.CompilerParams(vmem_limit_bytes=VMEM_LIMIT),
    )(core, *mid)


def assemble(result, tokens_grad, core, late, feed):
    mix_w, out_w, up_w, down_w = feed
    _, chans, ff = up_w.shape
    smem = pl.BlockSpec(memory_space=pltpu.SMEM)
    shapes = [
        (4, 3, 3, chans), (4, chans), (4, chans), (3, chans), (1, chans),
        (2, chans), (3, chans), (2, chans), (2, ff), (2, chans),
    ]

    def fixed(shape):
        return pl.BlockSpec(shape, lambda i: (0,) * len(shape))

    mix_w, out_w, conv_w, conv_b, gain, shift, last_shift, win_b, chan_b, out_b, up_b, down_b = pl.pallas_call(
        late_kernel,
        grid=(1,),
        in_specs=[smem] + [fixed(x.shape) for x in late] + [pl.BlockSpec(memory_space=pl.ANY)] * 2,
        out_specs=[fixed((1,) + x[1:]) for x in (mix_w.shape, out_w.shape)] + [fixed(x) for x in shapes],
        out_shape=[jax.ShapeDtypeStruct(x, F32) for x in (mix_w.shape, out_w.shape, *shapes)],
        input_output_aliases={3: 0, 4: 1},
        scratch_shapes=[pltpu.VMEM((SMALL_ROWS, chans), F32)],
        compiler_params=pltpu.CompilerParams(vmem_limit_bytes=VMEM_LIMIT),
    )(core, *late, mix_w, out_w)
    return (
        result, tokens_grad, conv_w, conv_b, gain, shift, last_shift.reshape(-1), mix_w,
        win_b.reshape(-1), chan_b.reshape(-1), out_w, out_b, up_w, up_b, down_w, down_b,
    )


def widen_kernel(here, *refs):
    out = refs[-1]
    cols = out.shape[2]
    for step, part in enumerate(refs[:-1]):

        @pl.when(pl.program_id(0) == step)
        def _():
            out[0] = part[:, :cols, :].astype(F32)


def widen(parts, here, cols):
    images = len(parts)
    height, width, chans = parts[0].shape
    return pl.pallas_call(
        widen_kernel,
        grid_spec=pltpu.PrefetchScalarGridSpec(
            num_scalar_prefetch=1,
            grid=(images,),
            in_specs=[pl.BlockSpec(x.shape, lambda i, at: (0, 0, 0), pipeline_mode=pl.Buffered(1)) for x in parts],
            out_specs=pl.BlockSpec(
                (1, height, cols, chans), lambda i, at: ((at[0] + images - i) % images, 0, 0, 0)
            ),
        ),
        out_shape=jax.ShapeDtypeStruct((images, height, cols, chans), F32),
        compiler_params=pltpu.CompilerParams(vmem_limit_bytes=VMEM_LIMIT),
    )(here.astype(jnp.int32).reshape(1), *parts)


def local(
    tokens, heights, conv_weight, conv_bias, norm_gain, norm_shift, mix_weight, window_bias, channel_bias,
    out_weight, out_bias, up_weight, up_bias, down_weight, down_bias, cotangent,
):
    images, height, cols, chans = tokens.shape
    count = lax.axis_size("rows")
    place = lax.axis_index("rows")
    width = -(-cols // 8) * 8
    groups = count // images
    members = [[g * images + j for j in range(images)] for g in range(groups)]
    rows_here = images * height
    level = lax.dynamic_index_in_dim(heights, place % images, 0, keepdims=False)
    open_rows = heights * 7 - place * height

    def gather_image(field):
        inside = jnp.arange(height, dtype=jnp.int32)[None, :] < open_rows[:, None]
        field = jnp.where(inside[:, :, None, None], field, jnp.zeros((), field.dtype))
        field = jnp.pad(field, ((0, 0), (0, 0), (0, width - cols), (0, 0)))
        field = lax.all_to_all(field, "rows", 0, 0, axis_index_groups=members, tiled=True)
        return field.reshape(rows_here, width, chans)

    def scatter_image(field):
        field = field.reshape(images, height, width, chans)
        field = lax.all_to_all(field, "rows", 0, 0, axis_index_groups=members, tiled=True)
        return field[:, :, :cols]

    def halo_of(field):
        flat = field.reshape(rows_here * width, chans)
        if groups == 1:
            return jnp.zeros((2 * width, chans), F32)
        down = [(i, i + images) for i in range(count - images)]
        up = [(i + images, i) for i in range(count - images)]
        above = lax.ppermute(flat[-width:].astype(BF16), "rows", down)
        below = lax.ppermute(flat[:width].astype(BF16), "rows", up)
        return jnp.concatenate([above, below], axis=0).astype(F32)

    def across(value):
        if groups == 1:
            return value
        other = [[j + g * images for g in range(groups)] for j in range(images)]
        return lax.psum(value, "rows", axis_index_groups=other)

    row = jnp.arange(rows_here * width, dtype=jnp.int32) // width + place // images * rows_here
    col = jnp.arange(rows_here * width, dtype=jnp.int32) % width
    mask = ((row < level * 7) & (col < cols)).astype(F32)
    mask = jnp.broadcast_to(mask[:, None], (rows_here * width, LANES))
    scale = lax.rsqrt((level * 7 * cols).astype(F32))
    scale = jnp.broadcast_to(scale, (8, LANES))
    x0 = gather_image(tokens)
    cot = gather_image(cotangent).reshape(rows_here * width, chans)

    def exchange(part, axis, step):
        size = lax.axis_size(axis)
        return lax.ppermute(part, axis, [(i, i ^ step) for i in range(size)])

    core = lax.axis_index("core").astype(jnp.int32).reshape(1)

    def share_cores(kept, sent):
        return (kept.astype(F32) + exchange(sent, "core", 1).astype(F32)).astype(BF16)

    def share(part, axis):
        size, me = lax.axis_size(axis), lax.axis_index(axis)
        rows = part.shape[0] // size

        def piece(step):
            return lax.dynamic_slice_in_dim(part, (me ^ step) * rows, rows, 0)

        total = piece(0).astype(F32)
        for step in range(1, size):
            total = total + exchange(piece(step), axis, step).astype(F32)
        return total.astype(BF16)

    def gather(part, axis):
        size, me = lax.axis_size(axis), lax.axis_index(axis)
        rows = part.shape[0]
        out = jnp.zeros((size * rows, part.shape[1]), part.dtype)
        for step in range(size):
            got = part if step == 0 else exchange(part, axis, step)
            out = lax.dynamic_update_slice_in_dim(out, got, (me ^ step) * rows, 0)
        return out

    def send_tokens(field):
        field = field.reshape(images, height, width, chans)
        here = place % images
        parts = []
        for step in range(images):
            part = lax.dynamic_index_in_dim(field, (here + step) % images, 0, keepdims=False)
            if step:
                pairs = [(g * images + j, g * images + (j + step) % images) for g in range(groups) for j in range(images)]
                part = lax.ppermute(part, "rows", pairs)
            parts.append(part)
        return parts

    weights = (
        conv_weight, conv_bias, norm_gain, norm_shift, mix_weight, window_bias, channel_bias,
        out_weight, out_bias, up_weight, up_bias, down_weight, down_bias,
    )
    result, tokens_grad, mid, kept, sent = image_block(
        x0, cot, halo_of(x0), mask, scale, halo_of, across, weights, cols, core,
        scatter_image, share_cores, lambda part: share(part, "plane"),
    )
    together = lax.optimization_barrier
    tokens_grad = send_tokens(tokens_grad)
    mid = share(mid, "rows")
    late = share_cores(kept, sent)
    late, mid = together((late, mid))
    late, mid = share(late, "plane"), gather(mid, "rows")
    late, mid = together((late, mid))
    late, mid = share(late, "rows"), gather(mid, "plane")
    late, mid, tokens_grad = together((late, mid, tokens_grad))
    late, mid = gather(late, "rows"), (mid, exchange(mid, "core", 1))
    tokens_grad = widen(tokens_grad, place % images, cols)
    late, mid, tokens_grad = together((late, mid, tokens_grad))
    late, feed = gather(late, "plane"), feed_grads(core, mid, chans, up_weight.shape[2])
    late, feed = together((late, feed))
    return assemble(result, tokens_grad, core, (late, exchange(late, "core", 1)), feed)


def solution(mesh):
    planes = mesh.shape["dp"] // 2
    fine = Mesh(mesh.devices.reshape(planes, 2, mesh.shape["rows"]), ("plane", "core", "rows"))
    dp = ("plane", "core")
    split = P(dp, "rows", None, None)
    in_specs = (split, P(dp)) + (P(),) * 13 + (split,)
    out_specs = (split, split) + (P(),) * 14
    return jax.shard_map(local, mesh=fine, in_specs=in_specs, out_specs=out_specs, check_vma=False)
```

time: 1490 us -> 428 us (0.29)
  local copies, waits for them, and re-layouts: 496 us -> 35.9 us
  waiting for transfers between devices: 466 us -> 76.7 us
  matrix products: 280 us -> 0 us
  Pallas kernels: 0 us -> 219 us
  other arithmetic: 172 us -> 18.1 us
  starting transfers between devices: 44.7 us -> 69.3 us
    psum x4 -> x0, waiting for transfers between devices: 447 us -> none  [the longest x2 366 us: local(): lax.psum((conv_w_grad, conv_b_grad, gain_grad, shift_grad, final_shift, m...]
    dot_general x35 -> x0, matrix products: 266 us -> none  [the longest x2 62.1 us: mlp_forward(): pre_act = jnp.dot(normed, up_w, preferred_element_type=jnp.float32) + up_b]
    reshape x28 -> x2, local copies, waits for them, and re-layouts: 233 us -> 2.57 us  [the longest x1 1.3 us: assemble(): chan_b.reshape(-1)]
    pallas_call x0 -> x14, Pallas kernels: none -> 219 us  [the longest x10 202 us: call(): pl.pallas_call(body, grid=(steps,), in_specs=[spec(block, index) for _, b...]
    reduce_sum x27 -> x0, other arithmetic: 95.3 us -> none  [the longest x4 16.4 us: layer_norm(): centre = value - jnp.mean(value, axis=-1, keepdims=True)]
    convert_element_type x13 -> x0, local copies, waits for them, and re-layouts: 59.4 us -> none  [the longest x4 34.3 us: channel_backward(): mixed_low = mixed_grad.astype(jnp.bfloat16)]
    another operation x66 -> x6, local copies, waits for them, and re-layouts: 50.4 us -> 0.79 us
    transpose x5 -> x0, local copies, waits for them, and re-layouts: 39.7 us -> none  [the longest x4 31.6 us: to_windows(): blocks.transpose(0, 1, 3, 5, 2, 4, 6).reshape(-1, HEADS, 49, HEAD_DIM)]
  transfers between devices with their start and end apart: 20 -> 34, of which waited for: 11 -> 14; matrix products, arithmetic and copies ran while one was open for 4% -> 7% of each run, Pallas kernels for 0% -> 32%
where the time goes in v1:
time: 428 us; the launch traced here: 422 us
  Pallas kernels  219 us (51%)
  waiting for transfers between devices  76.7 us (18%)
  starting transfers between devices  69.3 us (16%)
  local copies, waits for them, and re-layouts  35.9 us (8%)
  other arithmetic  18.1 us (4%)
    pallas_call x10, Pallas kernels, call(): pl.pallas_call(body, grid=(steps,), in_specs=[spec(block, index) for _, b...  202 us
    ppermute x28, starting transfers between devices, exchange(): return lax.ppermute(part, axis, [(i, i ^ step) for i in range(size)])  39 us
    ppermute x28, waiting for transfers between devices, exchange(): return lax.ppermute(part, axis, [(i, i ^ step) for i in range(size)])  35.4 us
    all_to_all x2, waiting for transfers between devices, gather_image(): lax.all_to_all(field, 'rows', 0, 0, axis_index_groups=members, tiled=True)  26.4 us
    ppermute x3, starting transfers between devices, send_tokens(): part = lax.ppermute(part, 'rows', pairs)  15.2 us
    unnamed x61, local copies, waits for them, and re-layouts  12.1 us
    all_to_all x2, starting transfers between devices, gather_image(): lax.all_to_all(field, 'rows', 0, 0, axis_index_groups=members, tiled=True)  10 us
  transfers between devices with their start and end apart: 34, of which 14 were waited for; matrix products, arithmetic and copies ran while one was open for 7% of the time, Pallas kernels for 32%

profile of v1, /device:TPU:0, one launch (start us, length us, event | category | flops | bytes accessed | tf_op | source)
XLA Modules:
  0.0 422.0 jit_solution(12552810090359928225)
XLA Ops:
  1.4 2.5 copy_select_fusion
  5.2 6.5 %all-to-all-start = ((bf16[4,7,72,384]{3,2,1,0:T(8,128)(2,1)}), bf16[4,7,72,384]{3,2,1,0:T(8,128)(2,1)S(1)}, u32[]{:S(2)}, u32[]{:S(2)}) async-start(bf16[4,7,72,384]{3,2,1,0:T(8,128)(2,1)} %pad.7), calls=%async_computation | async-start | bytes 3096576 | tf_op jit(solution)/shard_map/all_to_all | solution.py:1126
  19.7 2.0 slice_bitcast_fusion.6
  21.7 26.4 %all-to-all-done = bf16[4,7,72,384]{3,2,1,0:T(8,128)(2,1)S(1)} async-done(((bf16[4,7,72,384]{3,2,1,0:T(8,128)(2,1)}), bf16[4,7,72,384]{3,2,1,0:T(8,128)(2,1)S(1)}, u32[]{:S(2)}, u32[]{:S(2)}) %all-to-all-start) | async-done | bytes 1548320 | tf_op jit(solution)/shard_map/all_to_all | solution.py:1126
  48.1 3.6 all-to-all-start.1
  52.9 2.8 slice_bitcast_fusion.4
  55.7 1.6 slice_bitcast_fusion
  61.8 19.6 %shard_map.279 = (f32[2016,384]{1,0:T(8,128)}, bf16[2560,384]{1,0:T(8,128)(2,1)}, bf16[2560,1152]{1,0:T(8,128)(2,1)}, bf16[2560,384]{1,0:T(8,128)(2,1)}, f32[2016,384]{1,0:T(8,128)}) custom-call(bf16[28,72,384]{2,1,0:T(8,128)(2,1)} %bitcast.34, bf16[28,72,384]{2,1,0:T(8,128)(2,1)} %bitcast.35, bf16[28,72,384]{2,1,0:T(8,128)(2,1)} %bitcast.36, ...), custom_call_target="tpu_custom_call" | custom-call | flops 1 | bytes 1 | tf_op jit(solution)/shard_map/pallas_call | solution.py:580
  81.4 24.3 %shard_map.280 = (f32[2016,384]{1,0:T(8,128)}, f32[2016,384]{1,0:T(8,128)}, bf16[2016,384]{1,0:T(8,128)(2,1)}, bf16[2016,1536]{1,0:T(8,128)(2,1)}, bf16[2016,1536]{1,0:T(8,128)(2,1)}) custom-call(f32[2016,384]{1,0:T(8,128)} %get-tuple-element.98.refs_0_.refs_1_.refs_2_.refs_7_, f32[2016,384]{1,0:T(8,128)} %get-tuple-element.98.refs_0_.refs_1_.refs_2_.refs_7_, ...), custom_call_target="tpu_custom_call" | custom-call | flops 1 | bytes 1 | tf_op jit(solution)/shard_map/pallas_call | solution.py:580
  105.7 11.2 %shard_map.281 = (f32[2016,384]{1,0:T(8,128)}, bf16[2016,384]{1,0:T(8,128)(2,1)}, bf16[2016,1152]{1,0:T(8,128)(2,1)}, f32[3,128,128]{2,1,0:T(8,128)}) custom-call(f32[2016,384]{1,0:T(8,128)} %get-tuple-element.99.refs_0_.refs_1_.refs_2_.refs_7_, f32[2016,384]{1,0:T(8,128)} %get-tuple-element.99.refs_0_.refs_1_.refs_2_.refs_7_, ...), custom_call_target="tpu_custom_call" | custom-call | flops 1 | bytes 1 | tf_op jit(solution)/shard_map/pallas_call | solution.py:580
  117.5 6.6 %shard_map.282 = (bf16[2016,384]{1,0:T(8,128)(2,1)}, f32[2016,384]{1,0:T(8,128)}) custom-call(bf16[2016,1152]{1,0:T(8,128)(2,1)} %get-tuple-element.100.refs_0_.refs_7_.refs_1_, f32[3,128,128]{2,1,0:T(8,128)} %get-tuple-element.101.refs_1_.refs_2_, f32[8,128]{1,0:T(8,128)} %broadcast_in_dim.60.refs_2_.refs_4_, ...), custom_call_target="tpu_custom_call" | custom-call | flops 1 | bytes 1 | tf_op jit(solution)/shard_map/pallas_call | solution.py:580
  125.2 37.4 %shard_map.283 = (bf16[2016,384]{1,0:T(8,128)(2,1)}, f32[2016,384]{1,0:T(8,128)}, bf16[3072,384]{1,0:T(8,128)(2,1)}, f32[8,1536]{1,0:T(8,128)}, f32[24,384]{1,0:T(8,128)}) custom-call(f32[2016,384]{1,0:T(8,128)} %get-tuple-element.103.refs_0_.refs_1_.refs_2_.refs_6_, f32[2016,384]{1,0:T(8,128)} %get-tuple-element.103.refs_0_.refs_1_.refs_2_.refs_6_, ...), custom_call_target="tpu_custom_call" | custom-call | flops 1 | bytes 1 | tf_op jit(solution)/shard_map/pallas_call | solution.py:580
  162.6 5.1 %all-to-all-start.2 = ((bf16[4,7,72,384]{3,2,1,0:T(8,128)(2,1)}), bf16[4,7,72,384]{3,2,1,0:T(8,128)(2,1)S(1)}, u32[]{:S(2)}, u32[]{:S(2)}) async-start(bf16[4,7,72,384]{3,2,1,0:T(8,128)(2,1)} %bitcast.41), calls=%async_computation.2 | async-start | bytes 3096576 | tf_op jit(solution)/shard_map/all_to_all | solution.py:1131
  167.7 13.0 %shard_map.284 = (f32[2016,384]{1,0:T(8,128)}, bf16[2016,384]{1,0:T(8,128)(2,1)}, f32[3,128,128]{2,1,0:T(8,128)}, bf16[384,384]{1,0:T(8,128)(2,1)}, f32[72,384]{1,0:T(8,128)}, /*index=5*/f32[16,384]{1,0:T(8,128)}) custom-call(f32[2016,384]{1,0:T(8,128)} %get-tuple-element.105.refs_0_.refs_1_.refs_2_, f32[2016,384]{1,0:T(8,128)} %get-tuple-element.105.refs_0_.refs_1_.refs_2_, ...), custom_call_target="tpu_custom_call" | custom-call | flops 1 | bytes 1 | tf_op jit(solution)/shard_map/pallas_call | solution.py:580
  180.7 15.6 %shard_map.285 = (f32[2016,384]{1,0:T(8,128)}, bf16[1152,384]{1,0:T(8,128)(2,1)}, f32[8,1152]{1,0:T(8,128)}, f32[16,384]{1,0:T(8,128)}) custom-call(bf16[2016,384]{1,0:T(8,128)(2,1)} %get-tuple-element.107.refs_0_, bf16[2016,1152]{1,0:T(8,128)(2,1)} %get-tuple-element.100.refs_0_.refs_7_.refs_1_, f32[3,128,128]{2,1,0:T(8,128)} %get-tuple-element.101.refs_1_.refs_2_, ...), custom_call_target="tpu_custom_call" | custom-call | flops 1 | bytes 1 | tf_op jit(solution)/shard_map/pallas_call | solution.py:580
  196.3 6.8 %all-to-all-done.2 = bf16[4,7,72,384]{3,2,1,0:T(8,128)(2,1)S(1)} async-done(((bf16[4,7,72,384]{3,2,1,0:T(8,128)(2,1)}), bf16[4,7,72,384]{3,2,1,0:T(8,128)(2,1)S(1)}, u32[]{:S(2)}, u32[]{:S(2)}) %all-to-all-start.2) | async-done | bytes 1548320 | tf_op jit(solution)/shard_map/all_to_all | solution.py:1131
  204.2 32.1 %shard_map.286 = (f32[2016,384]{1,0:T(8,128)}, bf16[3840,384]{1,0:T(8,128)(2,1)}, bf16[3840,384]{1,0:T(8,128)(2,1)}, f32[8,1536]{1,0:T(8,128)}, f32[72,384]{1,0:T(8,128)}, /*index=5*/f32[32,384]{1,0:T(8,128)}) custom-call(f32[2016,384]{1,0:T(8,128)} %get-tuple-element.111.refs_0_.refs_1_.refs_2_, f32[2016,384]{1,0:T(8,128)} %get-tuple-element.111.refs_0_.refs_1_.refs_2_, ...), custom_call_target="tpu_custom_call" | custom-call | flops 1 | bytes 1 | tf_op jit(solution)/shard_map/pallas_call | solution.py:580
  236.4 5.6 %collective-permute-done = bf16[3840,384]{1,0:T(8,128)(2,1)S(1)} collective-permute-done((bf16[3840,384]{1,0:T(8,128)(2,1)}, bf16[3840,384]{1,0:T(8,128)(2,1)S(1)}, u32[]{:S(2)}, u32[]{:S(2)}) %collective-permute-start) | collective-permute-done | bytes 2949152 | tf_op jit(solution)/shard_map/ppermute | solution.py:1161
  242.0 1.6 copy-done.7
  243.5 3.5 add_convert_fusion
  252.0 33.9 %shard_map.287 = (f32[2016,384]{1,0:T(8,128)}, bf16[1536,384]{1,0:T(8,128)(2,1)}, f32[8,1152]{1,0:T(8,128)}, f32[72,384]{1,0:T(8,128)}, f32[32,384]{1,0:T(8,128)}) custom-call(f32[2016,384]{1,0:T(8,128)} %get-tuple-element.119.refs_0_.refs_1_.refs_2_, f32[2016,384]{1,0:T(8,128)} %get-tuple-element.119.refs_0_.refs_1_.refs_2_, ...), custom_call_target="tpu_custom_call" | custom-call | flops 1 | bytes 1 | tf_op jit(solution)/shard_map/pallas_call | solution.py:580
  285.9 2.8 add_convert_fusion.1.refs_7_
  288.7 8.1 %shard_map.288 = (bf16[2016,384]{1,0:T(8,128)(2,1)}, f32[72,384]{1,0:T(8,128)}, f32[8,384]{1,0:T(8,128)}) custom-call(f32[2016,384]{1,0:T(8,128)} %get-tuple-element.125.refs_0_.refs_1_.refs_2_, f32[2016,384]{1,0:T(8,128)} %get-tuple-element.125.refs_0_.refs_1_.refs_2_, f32[2016,384]{1,0:T(8,128)} %get-tuple-element.125.refs_0_.refs_1_.refs_2_, ...), custom_call_target="tpu_custom_call" | custom-call | flops 1 | bytes 1 | tf_op jit(solution)/shard_map/pallas_call | solution.py:580
  296.8 3.3 shard_map.289
  300.3 2.0 collective-permute-start.6
  302.3 2.4 collective-permute-start.7
  304.6 5.4 %collective-permute-done.5 = bf16[240,384]{1,0:T(8,128)(2,1)S(1)} collective-permute-done((bf16[240,384]{1,0:T(8,128)(2,1)S(1)}, bf16[240,384]{1,0:T(8,128)(2,1)S(1)}, u32[]{:S(2)}, u32[]{:S(2)}) %collective-permute-start.5) | collective-permute-done | bytes 184352 | tf_op jit(solution)/shard_map/ppermute | solution.py:1161
  310.0 6.6 %collective-permute-done.6 = bf16[240,384]{1,0:T(8,128)(2,1)S(1)} collective-permute-done((bf16[240,384]{1,0:T(8,128)(2,1)S(1)}, bf16[240,384]{1,0:T(8,128)(2,1)S(1)}, u32[]{:S(2)}, u32[]{:S(2)}) %collective-permute-start.6) | collective-permute-done | bytes 184352 | tf_op jit(solution)/shard_map/ppermute | solution.py:1161
  318.7 2.4 collective-permute-start.10
  322.2 4.2 collective-permute-start.11
  327.1 1.8 collective-permute-start.13
  330.3 1.8 collective-permute-done.11
  332.2 9.6 %collective-permute-done.12 = bf16[240,384]{1,0:T(8,128)(2,1)S(1)} collective-permute-done((bf16[240,384]{1,0:T(8,128)(2,1)S(1)}, bf16[240,384]{1,0:T(8,128)(2,1)S(1)}, u32[]{:S(2)}, u32[]{:S(2)}) %collective-permute-start.12) | collective-permute-done | bytes 184352 | tf_op jit(solution)/shard_map/ppermute | solution.py:1161
  345.5 3.0 collective-permute-start.14
  350.4 1.6 collective-permute-start.16
  352.5 1.8 collective-permute-done.15
  354.3 2.5 collective-permute-done.16
  356.8 11.8 %collective-permute-start.21 = (bf16[7,72,384]{2,1,0:T(8,128)(2,1)S(1)}, bf16[7,72,384]{2,1,0:T(8,128)(2,1)S(1)}, u32[]{:S(2)}, u32[]{:S(2)}) collective-permute-start(bf16[7,72,384]{2,1,0:T(8,128)(2,1)S(1)} %get-tuple-element.242), channel_id=1, source_target_pairs={{0,2},{1,3},{2,0},{3,1},{4,6},{5,7},{6,4},{7,5},{8,10},{9,11},{10,... | collective-permute-start | bytes 1161224 | tf_op jit(solution)/shard_map/ppermute | solution.py:1197
  369.4 3.4 collective-permute-start.22
  374.4 8.2 %collective-permute-done.21.refs_2_ = bf16[7,72,384]{2,1,0:T(8,128)(2,1)S(1)} collective-permute-done((bf16[7,72,384]{2,1,0:T(8,128)(2,1)S(1)}, bf16[7,72,384]{2,1,0:T(8,128)(2,1)S(1)}, u32[]{:S(2)}, u32[]{:S(2)}) %collective-permute-start.21) | collective-permute-done | bytes 387104 | tf_op jit(solution)/shard_map/ppermute | solution.py:1197
  382.7 7.2 %collective-permute-start.23 = (bf16[56,384]{1,0:T(8,128)(2,1)S(1)}, bf16[56,384]{1,0:T(8,128)(2,1)S(1)}, u32[]{:S(2)}, u32[]{:S(2)}) collective-permute-start(bf16[56,384]{1,0:T(8,128)(2,1)S(1)} %add_convert_fusion.5), channel_id=1, source_target_pairs={{0,1},{1,0},{2,3},{3,2},{4,5},{5,4},{6,7},{7,6},{8,9},{9,8},{10,11... | collective-permute-start | bytes 129032 | tf_op jit(solution)/shard_map/ppermute | solution.py:1161
  390.3 2.0 collective-permute-start.25
  392.4 3.6 shard_map.290
  396.3 1.6 collective-permute-start.27
  399.9 7.6 %shard_map.291 = (f32[2,384,1152]{2,1,0:T(8,128)}, f32[2,384,384]{2,1,0:T(8,128)}, f32[2,384,1536]{2,1,0:T(8,128)}, f32[2,1536,384]{2,1,0:T(8,128)}) custom-call(s32[1]{0:T(128)} %bitcast.13.refs_17_.core, bf16[3840,384]{1,0:T(8,128)(2,1)} %copy-done.4, bf16[3840,384]{1,0:T(8,128)(2,1)} %collective-permute-done.26.mid_b), custom_call_target="tpu_custom_call" | custom-call | tf_op jit(solution)/shard_map/pallas_call | solution.py:1040
  407.8 1.7 copy.48
  410.2 2.4 copy.49
  413.5 2.9 shard_map.292
  (171 shorter events, 46.3 us)
Async XLA Ops:
  3.8 7.8 %copy-start.28 = (s32[4]{0:T(128)S(1)}, s32[4]{0:T(128)}, u32[]{:S(2)}) copy-start(s32[4]{0:T(128)} %param.17) | copy-start | bytes 52
  3.9 8.4 %copy-start.19 = (bf16[4,3,3,384]{3,0,2,1:T(4,128)(2,1)S(1)}, bf16[4,3,3,384]{3,0,2,1:T(4,128)(2,1)}, u32[]{:S(2)}) copy-start(bf16[4,3,3,384]{3,0,2,1:T(4,128)(2,1)} %param.18) | copy-start | bytes 82948
  5.2 8.0 %copy-start.27 = (bf16[768]{0:T(1024)(128)(2,1)S(1)}, bf16[768]{0:T(1024)(128)(2,1)}, u32[]{:S(2)}) copy-start(bf16[768]{0:T(1024)(128)(2,1)} %param.23) | copy-start | bytes 4612
  5.2 8.1 %copy-start.25 = (bf16[2,384]{1,0:T(2,128)(2,1)S(1)}, bf16[2,384]{1,0:T(2,128)(2,1)}, u32[]{:S(2)}) copy-start(bf16[2,384]{1,0:T(2,128)(2,1)} %param.30) | copy-start | bytes 4612
  5.2 9.4 %copy-start.26 = (bf16[1152]{0:T(1024)(128)(2,1)S(1)}, bf16[1152]{0:T(1024)(128)(2,1)}, u32[]{:S(2)}) copy-start(bf16[1152]{0:T(1024)(128)(2,1)} %param.24) | copy-start | bytes 6916
  5.2 42.9 %all-to-all-start = ((bf16[4,7,72,384]{3,2,1,0:T(8,128)(2,1)}), bf16[4,7,72,384]{3,2,1,0:T(8,128)(2,1)S(1)}, u32[]{:S(2)}, u32[]{:S(2)}) async-start(bf16[4,7,72,384]{3,2,1,0:T(8,128)(2,1)} %pad.7), calls=%async_computation | async-start | bytes 3096576 | tf_op jit(solution)/shard_map/all_to_all | solution.py:1126
  18.6 33.7 %copy-start.20 = (bf16[2,1536]{1,0:T(2,128)(2,1)S(1)}, bf16[2,1536]{1,0:T(2,128)(2,1)}, u32[]{:S(2)}) copy-start(bf16[2,1536]{1,0:T(2,128)(2,1)} %param.28) | copy-start | bytes 18436
  48.1 75.9 %all-to-all-start.1 = ((bf16[4,7,72,384]{3,2,1,0:T(8,128)(2,1)}), bf16[4,7,72,384]{3,2,1,0:T(8,128)(2,1)S(1)}, u32[]{:S(2)}, u32[]{:S(2)}) async-start(bf16[4,7,72,384]{3,2,1,0:T(8,128)(2,1)} %pad.8), calls=%async_computation.1 | async-start | bytes 3096576 | tf_op jit(solution)/shard_map/all_to_all | solution.py:1126
  162.6 40.4 %all-to-all-start.2 = ((bf16[4,7,72,384]{3,2,1,0:T(8,128)(2,1)}), bf16[4,7,72,384]{3,2,1,0:T(8,128)(2,1)S(1)}, u32[]{:S(2)}, u32[]{:S(2)}) async-start(bf16[4,7,72,384]{3,2,1,0:T(8,128)(2,1)} %bitcast.41), calls=%async_computation.2 | async-start | bytes 3096576 | tf_op jit(solution)/shard_map/all_to_all | solution.py:1131
  236.3 5.7 %collective-permute-start = (bf16[3840,384]{1,0:T(8,128)(2,1)}, bf16[3840,384]{1,0:T(8,128)(2,1)S(1)}, u32[]{:S(2)}, u32[]{:S(2)}) collective-permute-start(bf16[3840,384]{1,0:T(8,128)(2,1)} %get-tuple-element.127), channel_id=1, source_target_pairs={{0,4},{4,0},{1,5},{5,1},{2,6},{6,2},{3,7},{7,3},{8,12},{12,8},{9,1... | collective-permute-start | bytes 8847368 | tf_op jit(solution)/shard_map/ppermute | solution.py:1161
  248.5 37.4 %collective-permute-start.1 = (bf16[960,384]{1,0:T(8,128)(2,1)}, bf16[960,384]{1,0:T(8,128)(2,1)}, u32[]{:S(2)}, u32[]{:S(2)}) collective-permute-start(bf16[960,384]{1,0:T(8,128)(2,1)} %get-tuple-element.232), channel_id=1, source_target_pairs={{0,8},{8,0},{16,24},{24,16},{1,9},{9,1},{17,25},{25,17},{2,10},{10... | collective-permute-start | bytes 2211848 | tf_op jit(solution)/shard_map/ppermute | solution.py:1161
  250.0 35.9 %collective-permute-start.2 = (bf16[960,384]{1,0:T(8,128)(2,1)}, bf16[960,384]{1,0:T(8,128)(2,1)}, u32[]{:S(2)}, u32[]{:S(2)}) collective-permute-start(bf16[960,384]{1,0:T(8,128)(2,1)} %get-tuple-element.234), channel_id=1, source_target_pairs={{0,16},{8,24},{16,0},{24,8},{1,17},{9,25},{17,1},{25,9},{2,18},{10... | collective-permute-start | bytes 2211848 | tf_op jit(solution)/shard_map/ppermute | solution.py:1161
  251.5 34.4 %collective-permute-start.3 = (bf16[960,384]{1,0:T(8,128)(2,1)}, bf16[960,384]{1,0:T(8,128)(2,1)}, u32[]{:S(2)}, u32[]{:S(2)}) collective-permute-start(bf16[960,384]{1,0:T(8,128)(2,1)} %get-tuple-element.233), channel_id=1, source_target_pairs={{0,24},{8,16},{16,8},{24,0},{1,25},{9,17},{17,9},{25,1},{2,26},{10... | collective-permute-start | bytes 2211848 | tf_op jit(solution)/shard_map/ppermute | solution.py:1161
  300.1 17.6 %copy-start.13 = (bf16[896,384]{1,0:T(8,128)(2,1)S(1)}, bf16[896,384]{1,0:T(8,128)(2,1)}, u32[]{:S(2)}) copy-start(bf16[896,384]{1,0:T(8,128)(2,1)} %get-tuple-element.142) | copy-start | bytes 2064388
  300.1 17.6 %collective-permute-start.4 = (bf16[896,384]{1,0:T(8,128)(2,1)}, bf16[896,384]{1,0:T(8,128)(2,1)S(1)}, u32[]{:S(2)}, u32[]{:S(2)}) collective-permute-start(bf16[896,384]{1,0:T(8,128)(2,1)} %get-tuple-element.143), channel_id=1, source_target_pairs={{0,4},{4,0},{1,5},{5,1},{2,6},{6,2},{3,7},{7,3},{8,12},{12,8},{9,1... | collective-permute-start | bytes 2064392 | tf_op jit(solution)/shard_map/ppermute | solution.py:1161
  300.2 9.8 %collective-permute-start.5 = (bf16[240,384]{1,0:T(8,128)(2,1)S(1)}, bf16[240,384]{1,0:T(8,128)(2,1)S(1)}, u32[]{:S(2)}, u32[]{:S(2)}) collective-permute-start(bf16[240,384]{1,0:T(8,128)(2,1)S(1)} %get-tuple-element.245), channel_id=1, source_target_pairs={{0,1},{1,0},{2,3},{3,2},{4,5},{5,4},{6,7},{7,6},{8,9},{9,8},{10,11... | collective-permute-start | bytes 552968 | tf_op jit(solution)/shard_map/ppermute | solution.py:1161
  300.3 16.4 %collective-permute-start.6 = (bf16[240,384]{1,0:T(8,128)(2,1)S(1)}, bf16[240,384]{1,0:T(8,128)(2,1)S(1)}, u32[]{:S(2)}, u32[]{:S(2)}) collective-permute-start(bf16[240,384]{1,0:T(8,128)(2,1)S(1)} %get-tuple-element.247), channel_id=1, source_target_pairs={{0,2},{1,3},{2,0},{3,1},{4,6},{5,7},{6,4},{7,5},{8,10},{9,11},{10,... | collective-permute-start | bytes 552968 | tf_op jit(solution)/shard_map/ppermute | solution.py:1161
  302.3 14.3 %collective-permute-start.7 = (bf16[240,384]{1,0:T(8,128)(2,1)S(1)}, bf16[240,384]{1,0:T(8,128)(2,1)}, u32[]{:S(2)}, u32[]{:S(2)}) collective-permute-start(bf16[240,384]{1,0:T(8,128)(2,1)S(1)} %get-tuple-element.246), channel_id=1, source_target_pairs={{0,3},{1,2},{2,1},{3,0},{4,7},{5,6},{6,5},{7,4},{8,11},{9,10},{10,... | collective-permute-start | bytes 552968 | tf_op jit(solution)/shard_map/ppermute | solution.py:1161
  317.9 30.6 %copy-start.11 = (bf16[2016,384]{1,0:T(8,128)(2,1)S(1)}, bf16[2016,384]{1,0:T(8,128)(2,1)}, u32[]{:S(2)}) copy-start(bf16[2016,384]{1,0:T(8,128)(2,1)} %get-tuple-element.148) | copy-start | bytes 4644868
  318.7 8.4 %collective-permute-start.10 = (bf16[224,384]{1,0:T(8,128)(2,1)}, bf16[224,384]{1,0:T(8,128)(2,1)S(1)}, u32[]{:S(2)}, u32[]{:S(2)}) collective-permute-start(bf16[224,384]{1,0:T(8,128)(2,1)} %get-tuple-element.249), channel_id=1, source_target_pairs={{0,24},{8,16},{16,8},{24,0},{1,25},{9,17},{17,9},{25,1},{2,26},{10... | collective-permute-start | bytes 516104 | tf_op jit(solution)/shard_map/ppermute | solution.py:1161
  321.1 8.0 %collective-permute-start.8 = (bf16[224,384]{1,0:T(8,128)(2,1)}, bf16[224,384]{1,0:T(8,128)(2,1)}, u32[]{:S(2)}, u32[]{:S(2)}) collective-permute-start(bf16[224,384]{1,0:T(8,128)(2,1)} %get-tuple-element.248), channel_id=1, source_target_pairs={{0,8},{8,0},{16,24},{24,16},{1,9},{9,1},{17,25},{25,17},{2,10},{10... | collective-permute-start | bytes 516104 | tf_op jit(solution)/shard_map/ppermute | solution.py:1161
  321.7 7.5 %collective-permute-start.9 = (bf16[224,384]{1,0:T(8,128)(2,1)}, bf16[224,384]{1,0:T(8,128)(2,1)}, u32[]{:S(2)}, u32[]{:S(2)}) collective-permute-start(bf16[224,384]{1,0:T(8,128)(2,1)} %get-tuple-element.250), channel_id=1, source_target_pairs={{0,16},{8,24},{16,0},{24,8},{1,17},{9,25},{17,1},{25,9},{2,18},{10... | collective-permute-start | bytes 516104 | tf_op jit(solution)/shard_map/ppermute | solution.py:1161
  322.2 9.9 %collective-permute-start.11 = (bf16[240,384]{1,0:T(8,128)(2,1)S(1)}, bf16[240,384]{1,0:T(8,128)(2,1)S(1)}, u32[]{:S(2)}, u32[]{:S(2)}) collective-permute-start(bf16[240,384]{1,0:T(8,128)(2,1)S(1)} %add_convert_fusion.3), channel_id=1, source_target_pairs={{0,1},{1,0},{2,3},{3,2},{4,5},{5,4},{6,7},{7,6},{8,9},{9,8},{10,11... | collective-permute-start | bytes 552968 | tf_op jit(solution)/shard_map/ppermute | solution.py:1161
  326.3 15.4 %collective-permute-start.12 = (bf16[240,384]{1,0:T(8,128)(2,1)S(1)}, bf16[240,384]{1,0:T(8,128)(2,1)S(1)}, u32[]{:S(2)}, u32[]{:S(2)}) collective-permute-start(bf16[240,384]{1,0:T(8,128)(2,1)S(1)} %add_convert_fusion.3), channel_id=1, source_target_pairs={{0,2},{1,3},{2,0},{3,1},{4,6},{5,7},{6,4},{7,5},{8,10},{9,11},{10,... | collective-permute-start | bytes 552968 | tf_op jit(solution)/shard_map/ppermute | solution.py:1161
  327.1 14.7 %collective-permute-start.13 = (bf16[240,384]{1,0:T(8,128)(2,1)S(1)}, bf16[240,384]{1,0:T(8,128)(2,1)S(1)}, u32[]{:S(2)}, u32[]{:S(2)}) collective-permute-start(bf16[240,384]{1,0:T(8,128)(2,1)S(1)} %add_convert_fusion.3), channel_id=1, source_target_pairs={{0,3},{1,2},{2,1},{3,0},{4,7},{5,6},{6,5},{7,4},{8,11},{9,10},{10,... | collective-permute-start | bytes 552968 | tf_op jit(solution)/shard_map/ppermute | solution.py:1161
  330.3 20.1 %copy-start.14 = (bf16[224,384]{1,0:T(8,128)(2,1)}, bf16[224,384]{1,0:T(8,128)(2,1)S(1)}, u32[]{:S(2)}) copy-start(bf16[224,384]{1,0:T(8,128)(2,1)S(1)} %add_convert_fusion.4) | copy-start | bytes 516100
  341.9 27.5 %collective-permute-start.17 = (bf16[960,384]{1,0:T(8,128)(2,1)S(1)}, bf16[960,384]{1,0:T(8,128)(2,1)}, u32[]{:S(2)}, u32[]{:S(2)}) collective-permute-start(bf16[960,384]{1,0:T(8,128)(2,1)S(1)} %constant_dynamic-update-slice_fusion.12), channel_id=1, source_target_pairs={{0,8},{8,0},{16,24},{24,16},{1,9},{9,1},{17,25},{25,17},{2,10},{10... | collective-permute-start | bytes 2211848 | tf_op jit(solution)/shard_map/ppermute | solution.py:1161
  343.4 30.6 %collective-permute-start.18 = (bf16[960,384]{1,0:T(8,128)(2,1)S(1)}, bf16[960,384]{1,0:T(8,128)(2,1)S(1)}, u32[]{:S(2)}, u32[]{:S(2)}) collective-permute-start(bf16[960,384]{1,0:T(8,128)(2,1)S(1)} %constant_dynamic-update-slice_fusion.12), channel_id=1, source_target_pairs={{0,16},{8,24},{16,0},{24,8},{1,17},{9,25},{17,1},{25,9},{2,18},{10... | collective-permute-start | bytes 2211848 | tf_op jit(solution)/shard_map/ppermute | solution.py:1161
  345.0 29.3 %collective-permute-start.19 = (bf16[960,384]{1,0:T(8,128)(2,1)S(1)}, bf16[960,384]{1,0:T(8,128)(2,1)S(1)}, u32[]{:S(2)}, u32[]{:S(2)}) collective-permute-start(bf16[960,384]{1,0:T(8,128)(2,1)S(1)} %constant_dynamic-update-slice_fusion.12), channel_id=1, source_target_pairs={{0,24},{8,16},{16,8},{24,0},{1,25},{9,17},{17,9},{25,1},{2,26},{10... | collective-permute-start | bytes 2211848 | tf_op jit(solution)/shard_map/ppermute | solution.py:1161
  345.5 5.0 %collective-permute-start.14 = (bf16[56,384]{1,0:T(8,128)(2,1)S(1)}, bf16[56,384]{1,0:T(8,128)(2,1)S(1)}, u32[]{:S(2)}, u32[]{:S(2)}) collective-permute-start(bf16[56,384]{1,0:T(8,128)(2,1)S(1)} %get-tuple-element.253), channel_id=1, source_target_pairs={{0,1},{1,0},{2,3},{3,2},{4,5},{5,4},{6,7},{7,6},{8,9},{9,8},{10,11... | collective-permute-start | bytes 129032 | tf_op jit(solution)/shard_map/ppermute | solution.py:1161
  349.4 4.9 %collective-permute-start.15 = (bf16[56,384]{1,0:T(8,128)(2,1)S(1)}, bf16[56,384]{1,0:T(8,128)(2,1)S(1)}, u32[]{:S(2)}, u32[]{:S(2)}) collective-permute-start(bf16[56,384]{1,0:T(8,128)(2,1)S(1)} %get-tuple-element.255), channel_id=1, source_target_pairs={{0,2},{1,3},{2,0},{3,1},{4,6},{5,7},{6,4},{7,5},{8,10},{9,11},{10,... | collective-permute-start | bytes 129032 | tf_op jit(solution)/shard_map/ppermute | solution.py:1161
  350.4 6.3 %collective-permute-start.16 = (bf16[56,384]{1,0:T(8,128)(2,1)S(1)}, bf16[56,384]{1,0:T(8,128)(2,1)S(1)}, u32[]{:S(2)}, u32[]{:S(2)}) collective-permute-start(bf16[56,384]{1,0:T(8,128)(2,1)S(1)} %get-tuple-element.254), channel_id=1, source_target_pairs={{0,3},{1,2},{2,1},{3,0},{4,7},{5,6},{6,5},{7,4},{8,11},{9,10},{10,... | collective-permute-start | bytes 129032 | tf_op jit(solution)/shard_map/ppermute | solution.py:1161
  354.3 20.1 %collective-permute-start.20 = (bf16[7,72,384]{2,1,0:T(8,128)(2,1)S(1)}, bf16[7,72,384]{2,1,0:T(8,128)(2,1)S(1)}, u32[]{:S(2)}, u32[]{:S(2)}) collective-permute-start(bf16[7,72,384]{2,1,0:T(8,128)(2,1)S(1)} %get-tuple-element.243), channel_id=1, source_target_pairs={{0,1},{1,2},{2,3},{3,0},{4,5},{5,6},{6,7},{7,4},{8,9},{9,10},{10,1... | collective-permute-start | bytes 1161224 | tf_op jit(solution)/shard_map/ppermute | solution.py:1197
  356.8 25.8 %collective-permute-start.21 = (bf16[7,72,384]{2,1,0:T(8,128)(2,1)S(1)}, bf16[7,72,384]{2,1,0:T(8,128)(2,1)S(1)}, u32[]{:S(2)}, u32[]{:S(2)}) collective-permute-start(bf16[7,72,384]{2,1,0:T(8,128)(2,1)S(1)} %get-tuple-element.242), channel_id=1, source_target_pairs={{0,2},{1,3},{2,0},{3,1},{4,6},{5,7},{6,4},{7,5},{8,10},{9,11},{10,... | collective-permute-start | bytes 1161224 | tf_op jit(solution)/shard_map/ppermute | solution.py:1197
  369.4 13.2 %collective-permute-start.22 = (bf16[7,72,384]{2,1,0:T(8,128)(2,1)S(1)}, bf16[7,72,384]{2,1,0:T(8,128)(2,1)S(1)}, u32[]{:S(2)}, u32[]{:S(2)}) collective-permute-start(bf16[7,72,384]{2,1,0:T(8,128)(2,1)S(1)} %get-tuple-element.241), channel_id=1, source_target_pairs={{0,3},{1,0},{2,1},{3,2},{4,7},{5,4},{6,5},{7,6},{8,11},{9,8},{10,9... | collective-permute-start | bytes 1161224 | tf_op jit(solution)/shard_map/ppermute | solution.py:1197
  374.4 21.6 %copy-start.4 = (bf16[3840,384]{1,0:T(8,128)(2,1)}, bf16[3840,384]{1,0:T(8,128)(2,1)S(1)}, u32[]{:S(2)}) copy-start(bf16[3840,384]{1,0:T(8,128)(2,1)S(1)} %constant_dynamic-update-slice_fusion.8.mid_a) | copy-start | bytes 8847364
  374.4 17.9 %copy-start.15 = (bf16[7,72,384]{2,1,0:T(8,128)(2,1)}, bf16[7,72,384]{2,1,0:T(8,128)(2,1)S(1)}, u32[]{:S(2)}) copy-start(bf16[7,72,384]{2,1,0:T(8,128)(2,1)S(1)} %collective-permute-done.20.refs_1_) | copy-start | bytes 1161220
  382.6 9.8 %copy-start.16 = (bf16[7,72,384]{2,1,0:T(8,128)(2,1)}, bf16[7,72,384]{2,1,0:T(8,128)(2,1)S(1)}, u32[]{:S(2)}) copy-start(bf16[7,72,384]{2,1,0:T(8,128)(2,1)S(1)} %collective-permute-done.21.refs_2_) | copy-start | bytes 1161220
  382.6 9.8 %copy-start.17 = (bf16[7,72,384]{2,1,0:T(8,128)(2,1)}, bf16[7,72,384]{2,1,0:T(8,128)(2,1)S(1)}, u32[]{:S(2)}) copy-start(bf16[7,72,384]{2,1,0:T(8,128)(2,1)S(1)} %collective-permute-done.22.refs_3_) | copy-start | bytes 1161220
  382.6 13.7 %collective-permute-start.26 = (bf16[3840,384]{1,0:T(8,128)(2,1)S(1)}, bf16[3840,384]{1,0:T(8,128)(2,1)}, u32[]{:S(2)}, u32[]{:S(2)}) collective-permute-start(bf16[3840,384]{1,0:T(8,128)(2,1)S(1)} %constant_dynamic-update-slice_fusion.8.mid_a), channel_id=1, source_target_pairs={{0,4},{4,0},{1,5},{5,1},{2,6},{6,2},{3,7},{7,3},{8,12},{12,8},{9,1... | collective-permute-start | bytes 8847368 | tf_op jit(solution)/shard_map/ppermute | solution.py:1161
  382.7 13.3 %collective-permute-start.23 = (bf16[56,384]{1,0:T(8,128)(2,1)S(1)}, bf16[56,384]{1,0:T(8,128)(2,1)S(1)}, u32[]{:S(2)}, u32[]{:S(2)}) collective-permute-start(bf16[56,384]{1,0:T(8,128)(2,1)S(1)} %add_convert_fusion.5), channel_id=1, source_target_pairs={{0,1},{1,0},{2,3},{3,2},{4,5},{5,4},{6,7},{7,6},{8,9},{9,8},{10,11... | collective-permute-start | bytes 129032 | tf_op jit(solution)/shard_map/ppermute | solution.py:1161
  389.8 6.2 %collective-permute-start.24 = (bf16[56,384]{1,0:T(8,128)(2,1)S(1)}, bf16[56,384]{1,0:T(8,128)(2,1)S(1)}, u32[]{:S(2)}, u32[]{:S(2)}) collective-permute-start(bf16[56,384]{1,0:T(8,128)(2,1)S(1)} %add_convert_fusion.5), channel_id=1, source_target_pairs={{0,2},{1,3},{2,0},{3,1},{4,6},{5,7},{6,4},{7,5},{8,10},{9,11},{10,... | collective-permute-start | bytes 129032 | tf_op jit(solution)/shard_map/ppermute | solution.py:1161
  390.3 5.9 %collective-permute-start.25 = (bf16[56,384]{1,0:T(8,128)(2,1)S(1)}, bf16[56,384]{1,0:T(8,128)(2,1)S(1)}, u32[]{:S(2)}, u32[]{:S(2)}) collective-permute-start(bf16[56,384]{1,0:T(8,128)(2,1)S(1)} %add_convert_fusion.5), channel_id=1, source_target_pairs={{0,3},{1,2},{2,1},{3,0},{4,7},{5,6},{6,5},{7,4},{8,11},{9,10},{10,... | collective-permute-start | bytes 129032 | tf_op jit(solution)/shard_map/ppermute | solution.py:1161
  396.3 11.3 %collective-permute-start.27 = (bf16[224,384]{1,0:T(8,128)(2,1)S(1)}, bf16[224,384]{1,0:T(8,128)(2,1)S(1)}, u32[]{:S(2)}, u32[]{:S(2)}) collective-permute-start(bf16[224,384]{1,0:T(8,128)(2,1)S(1)} %constant_dynamic-update-slice_fusion.4), channel_id=1, source_target_pairs={{0,8},{8,0},{16,24},{24,16},{1,9},{9,1},{17,25},{25,17},{2,10},{10... | collective-permute-start | bytes 516104 | tf_op jit(solution)/shard_map/ppermute | solution.py:1161
  397.8 9.7 %collective-permute-start.28 = (bf16[224,384]{1,0:T(8,128)(2,1)S(1)}, bf16[224,384]{1,0:T(8,128)(2,1)S(1)}, u32[]{:S(2)}, u32[]{:S(2)}) collective-permute-start(bf16[224,384]{1,0:T(8,128)(2,1)S(1)} %constant_dynamic-update-slice_fusion.4), channel_id=1, source_target_pairs={{0,16},{8,24},{16,0},{24,8},{1,17},{9,25},{17,1},{25,9},{2,18},{10... | collective-permute-start | bytes 516104 | tf_op jit(solution)/shard_map/ppermute | solution.py:1161
  399.3 8.3 %collective-permute-start.29 = (bf16[224,384]{1,0:T(8,128)(2,1)S(1)}, bf16[224,384]{1,0:T(8,128)(2,1)S(1)}, u32[]{:S(2)}, u32[]{:S(2)}) collective-permute-start(bf16[224,384]{1,0:T(8,128)(2,1)S(1)} %constant_dynamic-update-slice_fusion.4), channel_id=1, source_target_pairs={{0,24},{8,16},{16,8},{24,0},{1,25},{9,17},{17,9},{25,1},{2,26},{10... | collective-permute-start | bytes 516104 | tf_op jit(solution)/shard_map/ppermute | solution.py:1161
  399.9 7.8 %copy-start.2 = (bf16[4,7,72,384]{3,2,1,0:T(8,128)(2,1)S(1)}, bf16[4,7,72,384]{3,2,1,0:T(8,128)(2,1)}, u32[]{:S(2)}) copy-start(bf16[4,7,72,384]{3,2,1,0:T(8,128)(2,1)} %copy-done.1) | copy-start | bytes 4644868
  407.7 4.9 %collective-permute-start.30 = (bf16[896,384]{1,0:T(8,128)(2,1)S(1)}, bf16[896,384]{1,0:T(8,128)(2,1)S(1)}, u32[]{:S(2)}, u32[]{:S(2)}) collective-permute-start(bf16[896,384]{1,0:T(8,128)(2,1)S(1)} %constant_dynamic-update-slice_fusion.late_a), channel_id=1, source_target_pairs={{0,4},{4,0},{1,5},{5,1},{2,6},{6,2},{3,7},{7,3},{8,12},{12,8},{9,1... | collective-permute-start | bytes 2064392 | tf_op jit(solution)/shard_map/ppermute | solution.py:1161
  (15 other events, 61.0 us)
